TPU v7x, 32 devices: a whole 2x2x4 slice. The times are simulated.
32 devices in a mesh: group: 4 (over x, core), blk: 2 (over y), head: 4 (over z).
Axes of the slice: x: 2, y: 2, z: 4, core: 2. Of those that a mesh axis runs over, the one named last changes fastest.
Arguments:
- latents: bfloat16 [4, 1024, 1024], P('group', 'blk'), may hold values from -6 to 6
- inputs: bfloat16 [4, 512, 1024], P('group', 'blk'), may hold values from -6 to 6
- latent_group: int32 [4, 1024], P('group', 'blk'), may hold values from 0 to 15
- latent_valid: int32 [4, 1024], P('group', 'blk'), may hold values 0 or 1
- input_group: int32 [4, 512], P('group', 'blk'), may hold values from 0 to 15
- input_valid: int32 [4, 512], P('group', 'blk'), may hold values 0 or 1
- gains: float32 [5, 1024], replicated, may hold values from 0.1 to 1.9
- w_q_cross: bfloat16 [1024, 1024], P(None, 'head'), may hold values from -0.1875 to 0.1875
- w_kv_cross: bfloat16 [1024, 2, 1024], P(None, None, 'head'), may hold values from -0.1875 to 0.1875
- w_o_cross: bfloat16 [1024, 1024], P(None, 'head'), may hold values from -1.5 to 1.5
- w_in_a: bfloat16 [1024, 4096], P(None, 'head'), may hold values from -0.1875 to 0.1875
- w_out_a: bfloat16 [1024, 4096], P(None, 'head'), may hold values from -0.09375 to 0.09375
- w_qkv_self: bfloat16 [1024, 3, 1024], P(None, None, 'head'), may hold values from -0.1875 to 0.1875
- w_o_self: bfloat16 [1024, 1024], P(None, 'head'), may hold values from -1.5 to 1.5
- w_in_b: bfloat16 [1024, 4096], P(None, 'head'), may hold values from -0.1875 to 0.1875
- w_out_b: bfloat16 [1024, 4096], P(None, 'head'), may hold values from -0.09375 to 0.09375
- out_grad: bfloat16 [4, 1024, 1024], P('group', 'blk'), may hold values from -6 to 6
Outputs:
- latents_out: bfloat16 [4, 1024, 1024], P('group', 'blk')
- latent_grad: float32 [4, 1024, 1024], P('group', 'blk')
- input_grad: float32 [4, 512, 1024], P('group', 'blk')
- gains_grad: float32 [5, 1024], replicated
- grad_w_q_cross: float32 [1024, 1024], P(None, 'head')
- grad_w_kv_cross: float32 [1024, 2, 1024], P(None, None, 'head')
- grad_w_o_cross: float32 [1024, 1024], P(None, 'head')
- grad_w_in_a: float32 [1024, 4096], P(None, 'head')
- grad_w_out_a: float32 [1024, 4096], P(None, 'head')
- grad_w_qkv_self: float32 [1024, 3, 1024], P(None, None, 'head')
- grad_w_o_self: float32 [1024, 1024], P(None, 'head')
- grad_w_in_b: float32 [1024, 4096], P(None, 'head')
- grad_w_out_b: float32 [1024, 4096], P(None, 'head')
Inputs may be any that keep to these rules, and one draw needn't show every extreme that they name: `latent_group`: a latent attends only to inputs and latents of its own group. `latent_valid`: padded tokens are never attended to as keys.
All inputs are finite; a program needn't handle non-finite values. No bound on the sum of `latent_valid` or of `input_valid` on one device may be relied on, other than what follows from the above.
Results may differ from a plain program's by a relative error of at most 0.024.
Values may be sent and summed in bfloat16 or wider, within the bound.
A program may use at most 192 MiB of HBM per device.

v0:
```python
import jax
import jax.numpy as jnp
from jax import lax
from jax.sharding import PartitionSpec as P

HEAD_DIM = 128


masked_fill = -1000.0
contract_last = (((1,), (1,)), ((), ()))


def layer_norm(values, gains_row):
    centred = values - jnp.mean(values, axis=-1, keepdims=True)
    variance = jnp.mean(centred * centred, axis=-1, keepdims=True)
    return centred * lax.rsqrt(variance + 1e-05) * gains_row


def norm_back(values, gains_row, cotangent):
    unused, pullback = jax.vjp(layer_norm, values, gains_row)
    return pullback(cotangent)


def out_product(left, right):
    return lax.dot_general(left, right, contract_last, preferred_element_type=jnp.float32)


def block_rows(item_count):
    if item_count > 1024 and item_count % 1024 == 0:
        return 1024
    return item_count


def head_sum(partial_sum):
    return lax.psum(partial_sum, "head")


def head_grad_sum(partial_sum):
    return lax.psum(partial_sum, "head")


def score_block(query_heads, key_heads, query_code, key_code):
    scores = jnp.einsum(
        "qhd,khd->hqk", query_heads, key_heads, preferred_element_type=jnp.float32
    ) * HEAD_DIM ** (-0.5)
    allowed = query_code[:, None] == key_code[None, :]
    return (jnp.where(allowed[None], scores, masked_fill), allowed)


def cycle_attend(queries, query_code, key_rows, value_rows, key_code):
    row_count = queries.shape[0]
    heads_local = queries.shape[1] // HEAD_DIM
    query_heads = queries.reshape(row_count, heads_local, HEAD_DIM)

    def stats_block(state_carry, block_data):
        running, totals = state_carry
        key_block, code_block = block_data
        key_heads = key_block.reshape(key_block.shape[0], heads_local, HEAD_DIM)
        scores, allowed = score_block(query_heads, key_heads, query_code, code_block)
        largest = jnp.maximum(running, jnp.max(scores, axis=-1))
        totals = totals * jnp.exp(running - largest) + jnp.sum(
            jnp.exp(scores - largest[:, :, None]), axis=-1
        )
        return ((largest, totals), None)

    stats_init = (
        jnp.full((heads_local, row_count), -jnp.inf, jnp.float32),
        jnp.zeros((heads_local, row_count), jnp.float32),
    )
    state_carry = stats_init
    key_piece = lax.all_gather(key_rows, "blk", axis=0, tiled=True)
    code_piece = lax.all_gather(key_code, "blk", axis=0, tiled=True)
    item_count = key_piece.shape[0]
    step_rows = block_rows(item_count)
    block_count = item_count // step_rows
    stacked = (
        key_piece.reshape(block_count, step_rows, key_piece.shape[1]),
        code_piece.reshape(block_count, step_rows),
    )
    state_carry, unused = lax.scan(stats_block, state_carry, stacked)
    running, totals = state_carry
    log_sums = running + jnp.log(totals)

    def one_block(accumulated, block_data):
        key_block, value_block, code_block = block_data
        key_heads = key_block.reshape(key_block.shape[0], heads_local, HEAD_DIM)
        value_heads = value_block.reshape(value_block.shape[0], heads_local, HEAD_DIM)
        scores, allowed = score_block(query_heads, key_heads, query_code, code_block)
        prob_rows = jnp.exp(scores - log_sums[:, :, None]).astype(jnp.bfloat16)
        accumulated = accumulated + jnp.einsum(
            "hqk,khd->qhd", prob_rows, value_heads, preferred_element_type=jnp.float32
        )
        return (accumulated, None)

    initial = jnp.zeros((row_count, heads_local, HEAD_DIM), jnp.float32)
    accumulated = initial
    key_piece = lax.all_gather(key_rows, "blk", axis=0, tiled=True)
    value_piece = lax.all_gather(value_rows, "blk", axis=0, tiled=True)
    code_piece = lax.all_gather(key_code, "blk", axis=0, tiled=True)
    item_count = key_piece.shape[0]
    step_rows = block_rows(item_count)
    block_count = item_count // step_rows
    stacked = (
        key_piece.reshape(block_count, step_rows, key_piece.shape[1]),
        value_piece.reshape(block_count, step_rows, value_piece.shape[1]),
        code_piece.reshape(block_count, step_rows),
    )
    accumulated, unused = lax.scan(one_block, accumulated, stacked)
    mixed = accumulated.reshape(row_count, heads_local * HEAD_DIM)
    return (mixed, log_sums)


def grad_parts(query_rows, grad_rows, query_code, log_sums, deltas, key_rows, value_rows, key_code):
    heads_local = query_rows.shape[1] // HEAD_DIM
    query_heads = query_rows.reshape(query_rows.shape[0], heads_local, HEAD_DIM)
    grad_heads = grad_rows.reshape(grad_rows.shape[0], heads_local, HEAD_DIM)
    key_heads = key_rows.reshape(key_rows.shape[0], heads_local, HEAD_DIM)
    value_heads = value_rows.reshape(value_rows.shape[0], heads_local, HEAD_DIM)
    scores, allowed = score_block(query_heads, key_heads, query_code, key_code)
    prob_rows = jnp.exp(scores - log_sums[:, :, None])
    grad_probs = jnp.einsum(
        "qhd,khd->hqk", grad_heads, value_heads, preferred_element_type=jnp.float32
    )
    grad_scores = jnp.where(
        allowed[None], prob_rows * (grad_probs - deltas[:, :, None]), 0.0
    ).astype(jnp.bfloat16)
    return (query_heads, grad_heads, key_heads, grad_scores, prob_rows)


def query_part(grad_scores, key_heads, row_shape):
    grad_query = jnp.einsum(
        "hqk,khd->qhd", grad_scores, key_heads, preferred_element_type=jnp.float32
    ) * HEAD_DIM ** (-0.5)
    return grad_query.reshape(row_shape)


def key_parts(grad_scores, prob_rows, query_heads, grad_heads, row_shape):
    grad_key = jnp.einsum(
        "hqk,qhd->khd", grad_scores, query_heads, preferred_element_type=jnp.float32
    ) * HEAD_DIM ** (-0.5)
    grad_value = jnp.einsum(
        "hqk,qhd->khd",
        prob_rows.astype(jnp.bfloat16),
        grad_heads,
        preferred_element_type=jnp.float32,
    )
    return (grad_key.reshape(row_shape), grad_value.reshape(row_shape))


def row_delta(grad_mixed, mixed):
    row_count = mixed.shape[0]
    heads_local = mixed.shape[1] // HEAD_DIM
    product = (grad_mixed.astype(jnp.float32) * mixed).reshape(row_count, heads_local, HEAD_DIM)
    return jnp.sum(product, axis=-1).T


def attend_back(queries, grad_mixed, query_code, log_sums, deltas, key_rows, value_rows, key_code):
    row_count = queries.shape[0]
    col_width = queries.shape[1]
    heads_local = col_width // HEAD_DIM
    all_keys, all_values, all_kcodes, all_queries, all_grads, all_qcodes = (
        lax.all_gather(key_rows, "blk", axis=0, tiled=True),
        lax.all_gather(value_rows, "blk", axis=0, tiled=True),
        lax.all_gather(key_code, "blk", axis=0, tiled=True),
        lax.all_gather(queries, "blk", axis=0, tiled=True),
        lax.all_gather(grad_mixed, "blk", axis=0, tiled=True),
        lax.all_gather(query_code, "blk", axis=0, tiled=True),
    )
    all_sums, all_deltas = (
        lax.all_gather(log_sums, "blk", axis=1, tiled=True),
        lax.all_gather(deltas, "blk", axis=1, tiled=True),
    )
    key_total = all_keys.shape[0]
    key_step = block_rows(key_total)
    key_blocks = key_total // key_step

    def own_queries(grad_query, block_data):
        key_block_rows, value_block_rows, code_block = block_data
        parts = grad_parts(
            queries,
            grad_mixed,
            query_code,
            log_sums,
            deltas,
            key_block_rows,
            value_block_rows,
            code_block,
        )
        return (grad_query + query_part(parts[3], parts[2], queries.shape), None)

    key_stack = (
        all_keys.reshape(key_blocks, key_step, col_width),
        all_values.reshape(key_blocks, key_step, col_width),
        all_kcodes.reshape(key_blocks, key_step),
    )
    grad_query, unused = lax.scan(
        own_queries, jnp.zeros((row_count, col_width), jnp.float32), key_stack
    )
    query_total = all_queries.shape[0]
    query_step = block_rows(query_total)
    query_blocks = query_total // query_step
    key_count = key_rows.shape[0]

    def own_keys(state_carry, block_data):
        grad_key, grad_value = state_carry
        query_block_rows, grad_block_rows, code_block, sums_block, deltas_block = block_data
        query_heads, grad_heads, key_heads, grad_scores, prob_rows = grad_parts(
            query_block_rows,
            grad_block_rows,
            code_block,
            sums_block,
            deltas_block,
            key_rows,
            value_rows,
            key_code,
        )
        part_key, part_value = key_parts(
            grad_scores, prob_rows, query_heads, grad_heads, key_rows.shape
        )
        return ((grad_key + part_key, grad_value + part_value), None)

    query_stack = (
        all_queries.reshape(query_blocks, query_step, col_width),
        all_grads.reshape(query_blocks, query_step, col_width),
        all_qcodes.reshape(query_blocks, query_step),
        all_sums.reshape(heads_local, query_blocks, query_step).transpose(1, 0, 2),
        all_deltas.reshape(heads_local, query_blocks, query_step).transpose(1, 0, 2),
    )
    zeros_keys = jnp.zeros((key_count, col_width), jnp.float32)
    (grad_key, grad_value), unused = lax.scan(own_keys, (zeros_keys, zeros_keys), query_stack)
    return (grad_query, grad_key, grad_value)


def mlp_forward(stream, gains_row, weight_in, weight_out):
    hidden_in = layer_norm(stream, gains_row).astype(jnp.bfloat16)
    hidden = jnp.dot(hidden_in, weight_in, preferred_element_type=jnp.float32)
    activated = jax.nn.gelu(hidden).astype(jnp.bfloat16)
    branch = head_sum(out_product(activated, weight_out))
    return (stream + branch, (hidden_in, hidden, activated))


def mlp_backward(stream, gains_row, weight_in, weight_out, saved, grad_stream):
    hidden_in, hidden, activated = saved
    grad_low = grad_stream.astype(jnp.bfloat16)
    grad_weight_out = jnp.einsum(
        "td,tf->df", grad_low, activated, preferred_element_type=jnp.float32
    )
    grad_activated = jnp.dot(grad_low, weight_out, preferred_element_type=jnp.float32)
    unused, gelu_back = jax.vjp(jax.nn.gelu, hidden)
    grad_hidden = gelu_back(grad_activated)[0].astype(jnp.bfloat16)
    grad_weight_in = jnp.einsum(
        "td,tf->df", hidden_in, grad_hidden, preferred_element_type=jnp.float32
    )
    grad_normed = head_grad_sum(out_product(grad_hidden, weight_in))
    grad_input, grad_gain = norm_back(stream, gains_row, grad_normed)
    return (grad_stream + grad_input, grad_gain, grad_weight_in, grad_weight_out)


def self_forward(stream, gains_row, weight_triple, weight_out, query_code, key_code):
    normed_low = layer_norm(stream, gains_row).astype(jnp.bfloat16)
    col_width = weight_triple.shape[2]
    triple = jnp.dot(
        normed_low,
        weight_triple.reshape(weight_triple.shape[0], 3 * col_width),
        preferred_element_type=jnp.float32,
    ).astype(jnp.bfloat16)
    queries = triple[:, :col_width]
    key_rows = triple[:, col_width : 2 * col_width]
    value_rows = triple[:, 2 * col_width :]
    mixed, log_sums = cycle_attend(queries, query_code, key_rows, value_rows, key_code)
    mixed_low = mixed.astype(jnp.bfloat16)
    branch = head_sum(out_product(mixed_low, weight_out))
    return (
        stream + branch,
        (normed_low, queries, key_rows, value_rows, mixed, mixed_low, log_sums),
    )


def self_backward(
    stream, gains_row, weight_triple, weight_out, saved, grad_stream, query_code, key_code
):
    normed_low, queries, key_rows, value_rows, mixed, mixed_low, log_sums = saved
    grad_low = grad_stream.astype(jnp.bfloat16)
    grad_weight_out = jnp.einsum(
        "td,ti->di", grad_low, mixed_low, preferred_element_type=jnp.float32
    )
    grad_mixed = jnp.dot(grad_low, weight_out, preferred_element_type=jnp.float32).astype(
        jnp.bfloat16
    )
    deltas = row_delta(grad_mixed, mixed)
    grad_query, grad_key, grad_value = attend_back(
        queries, grad_mixed, query_code, log_sums, deltas, key_rows, value_rows, key_code
    )
    grad_triple = jnp.concatenate([grad_query, grad_key, grad_value], axis=1).astype(jnp.bfloat16)
    grad_weight_triple = jnp.einsum(
        "td,tc->dc", normed_low, grad_triple, preferred_element_type=jnp.float32
    ).reshape(weight_triple.shape)
    grad_normed = head_grad_sum(
        out_product(grad_triple, weight_triple.reshape(weight_triple.shape[0], -1))
    )
    grad_input, grad_gain = norm_back(stream, gains_row, grad_normed)
    return (grad_stream + grad_input, grad_gain, grad_weight_triple, grad_weight_out)


def cross_forward(
    stream, input_rows, gains, weight_query, weight_pairs, weight_out, query_code, key_code
):
    latent_low = layer_norm(stream, gains[0]).astype(jnp.bfloat16)
    input_low = layer_norm(input_rows, gains[1]).astype(jnp.bfloat16)
    col_width = weight_query.shape[1]
    queries = jnp.dot(latent_low, weight_query, preferred_element_type=jnp.float32).astype(
        jnp.bfloat16
    )
    paired = jnp.dot(
        input_low,
        weight_pairs.reshape(weight_pairs.shape[0], 2 * col_width),
        preferred_element_type=jnp.float32,
    ).astype(jnp.bfloat16)
    key_rows = paired[:, :col_width]
    value_rows = paired[:, col_width:]
    mixed, log_sums = cycle_attend(queries, query_code, key_rows, value_rows, key_code)
    mixed_low = mixed.astype(jnp.bfloat16)
    branch = head_sum(out_product(mixed_low, weight_out))
    return (
        stream + branch,
        (latent_low, input_low, queries, key_rows, value_rows, mixed, mixed_low, log_sums),
    )


def cross_backward(
    stream,
    input_rows,
    gains,
    weight_query,
    weight_pairs,
    weight_out,
    saved,
    grad_stream,
    query_code,
    key_code,
):
    latent_low, input_low, queries, key_rows, value_rows, mixed, mixed_low, log_sums = saved
    grad_low = grad_stream.astype(jnp.bfloat16)
    grad_weight_out = jnp.einsum(
        "td,ti->di", grad_low, mixed_low, preferred_element_type=jnp.float32
    )
    grad_mixed = jnp.dot(grad_low, weight_out, preferred_element_type=jnp.float32).astype(
        jnp.bfloat16
    )
    deltas = row_delta(grad_mixed, mixed)
    grad_query, grad_key, grad_value = attend_back(
        queries, grad_mixed, query_code, log_sums, deltas, key_rows, value_rows, key_code
    )
    grad_query_low = grad_query.astype(jnp.bfloat16)
    grad_pairs = jnp.concatenate([grad_key, grad_value], axis=1).astype(jnp.bfloat16)
    grad_weight_query = jnp.einsum(
        "td,tc->dc", latent_low, grad_query_low, preferred_element_type=jnp.float32
    )
    grad_weight_pairs = jnp.einsum(
        "td,tc->dc", input_low, grad_pairs, preferred_element_type=jnp.float32
    ).reshape(weight_pairs.shape)
    latent_part = out_product(grad_query_low, weight_query)
    input_part = out_product(grad_pairs, weight_pairs.reshape(weight_pairs.shape[0], -1))
    latent_normed, input_normed = lax.psum((latent_part, input_part), "head")
    grad_latent, gain_zero = norm_back(stream, gains[0], latent_normed)
    grad_inputs, gain_one = norm_back(input_rows, gains[1], input_normed)
    return (
        grad_stream + grad_latent,
        grad_inputs,
        gain_zero,
        gain_one,
        grad_weight_query,
        grad_weight_pairs,
        grad_weight_out,
    )


def per_device(
    latents,
    inputs,
    latent_group,
    latent_valid,
    input_group,
    input_valid,
    gains,
    w_q_cross,
    w_kv_cross,
    w_o_cross,
    w_in_a,
    w_out_a,
    w_qkv_self,
    w_o_self,
    w_in_b,
    w_out_b,
    out_grad,
):
    start_stream = latents[0].astype(jnp.float32)
    input_rows = inputs[0].astype(jnp.float32)
    query_code = latent_group[0].astype(jnp.bfloat16)
    input_code = jnp.where(input_valid[0] == 1, input_group[0], -1).astype(jnp.bfloat16)
    self_code = jnp.where(latent_valid[0] == 1, latent_group[0], -1).astype(jnp.bfloat16)
    cross_stream, cross_saved = cross_forward(
        start_stream, input_rows, gains, w_q_cross, w_kv_cross, w_o_cross, query_code, input_code
    )
    middle_stream, first_saved = mlp_forward(cross_stream, gains[2], w_in_a, w_out_a)
    self_stream, self_saved = self_forward(
        middle_stream, gains[3], w_qkv_self, w_o_self, query_code, self_code
    )
    final_stream, second_saved = mlp_forward(self_stream, gains[4], w_in_b, w_out_b)
    grad_stream = out_grad[0].astype(jnp.float32)
    grad_stream, gain_four, grad_in_b, grad_out_b = mlp_backward(
        self_stream, gains[4], w_in_b, w_out_b, second_saved, grad_stream
    )
    grad_stream, gain_three, grad_qkv_self, grad_o_self = self_backward(
        middle_stream,
        gains[3],
        w_qkv_self,
        w_o_self,
        self_saved,
        grad_stream,
        query_code,
        self_code,
    )
    grad_stream, gain_two, grad_in_a, grad_out_a = mlp_backward(
        cross_stream, gains[2], w_in_a, w_out_a, first_saved, grad_stream
    )
    grad_stream, grad_inputs, gain_zero, gain_one, grad_q_cross, grad_kv_cross, grad_o_cross = (
        cross_backward(
            start_stream,
            input_rows,
            gains,
            w_q_cross,
            w_kv_cross,
            w_o_cross,
            cross_saved,
            grad_stream,
            query_code,
            input_code,
        )
    )
    gain_terms = jnp.stack([gain_zero, gain_one, gain_two, gain_three, gain_four], axis=1)
    (
        sum_gains,
        sum_q_cross,
        sum_kv_cross,
        sum_o_cross,
        sum_in_a,
        sum_out_a,
        sum_qkv_self,
        sum_o_self,
        sum_in_b,
        sum_out_b,
    ) = (
        lax.psum_scatter(gain_terms, ("group", "blk"), scatter_dimension=0, tiled=True),
        lax.psum_scatter(grad_q_cross, ("group", "blk"), scatter_dimension=0, tiled=True),
        lax.psum_scatter(grad_kv_cross, ("group", "blk"), scatter_dimension=0, tiled=True),
        lax.psum_scatter(grad_o_cross, ("group", "blk"), scatter_dimension=0, tiled=True),
        lax.psum_scatter(grad_in_a, ("group", "blk"), scatter_dimension=0, tiled=True),
        lax.psum_scatter(grad_out_a, ("group", "blk"), scatter_dimension=0, tiled=True),
        lax.psum_scatter(grad_qkv_self, ("group", "blk"), scatter_dimension=0, tiled=True),
        lax.psum_scatter(grad_o_self, ("group", "blk"), scatter_dimension=0, tiled=True),
        lax.psum_scatter(grad_in_b, ("group", "blk"), scatter_dimension=0, tiled=True),
        lax.psum_scatter(grad_out_b, ("group", "blk"), scatter_dimension=0, tiled=True),
    )
    (
        full_gains,
        full_q_cross,
        full_kv_cross,
        full_o_cross,
        full_in_a,
        full_out_a,
        full_qkv_self,
        full_o_self,
        full_in_b,
        full_out_b,
    ) = (
        lax.all_gather(sum_gains, ("group", "blk"), axis=0, tiled=True),
        lax.all_gather(sum_q_cross, ("group", "blk"), axis=0, tiled=True),
        lax.all_gather(sum_kv_cross, ("group", "blk"), axis=0, tiled=True),
        lax.all_gather(sum_o_cross, ("group", "blk"), axis=0, tiled=True),
        lax.all_gather(sum_in_a, ("group", "blk"), axis=0, tiled=True),
        lax.all_gather(sum_out_a, ("group", "blk"), axis=0, tiled=True),
        lax.all_gather(sum_qkv_self, ("group", "blk"), axis=0, tiled=True),
        lax.all_gather(sum_o_self, ("group", "blk"), axis=0, tiled=True),
        lax.all_gather(sum_in_b, ("group", "blk"), axis=0, tiled=True),
        lax.all_gather(sum_out_b, ("group", "blk"), axis=0, tiled=True),
    )
    return (
        final_stream.astype(jnp.bfloat16)[None],
        grad_stream[None],
        grad_inputs[None],
        full_gains.T,
        full_q_cross,
        full_kv_cross,
        full_o_cross,
        full_in_a,
        full_out_a,
        full_qkv_self,
        full_o_self,
        full_in_b,
        full_out_b,
    )


def solution(mesh):
    return jax.shard_map(
        per_device,
        mesh=mesh,
        in_specs=(
            P("group", "blk", None),
            P("group", "blk", None),
            P("group", "blk"),
            P("group", "blk"),
            P("group", "blk"),
            P("group", "blk"),
            P(),
            P(None, "head"),
            P(None, None, "head"),
            P(None, "head"),
            P(None, "head"),
            P(None, "head"),
            P(None, None, "head"),
            P(None, "head"),
            P(None, "head"),
            P(None, "head"),
            P("group", "blk", None),
        ),
        out_specs=(
            P("group", "blk", None),
            P("group", "blk", None),
            P("group", "blk", None),
            P(),
            P(None, "head"),
            P(None, None, "head"),
            P(None, "head"),
            P(None, "head"),
            P(None, "head"),
            P(None, None, "head"),
            P(None, "head"),
            P(None, "head"),
            P(None, "head"),
        ),
        check_vma=False,
    )
```

profile of v0, /device:TPU:0, one launch (start us, length us, event | category | flops | bytes accessed | tf_op | source)
XLA Modules:
  0.0 1653.8 jit_solution(13502047111145848297)
XLA Ops:
  11.3 7.1 all_gather.86
  42.3 88.1 %all-reduce.9.cloned.1.call-done = f32[512,1024]{1,0:T(8,128)} async-done(((f32[512,1024]{1,0:T(8,128)}), f32[512,1024]{1,0:T(8,128)}) %all-reduce.9.cloned.1.call-update) | async-done | bytes 2097168 | tf_op jit(solution)/shard_map/psum | solution.py:35
  148.3 77.4 %all-reduce.11.cloned.1.call-done = f32[512,1024]{1,0:T(8,128)} async-done(((f32[512,1024]{1,0:T(8,128)}), f32[512,1024]{1,0:T(8,128)}) %all-reduce.11.cloned.1.call-update) | async-done | bytes 2097168 | tf_op jit(solution)/shard_map/psum | solution.py:35
  233.2 8.8 all_gather.89
  244.0 8.2 all_gather.91
  262.7 86.0 %all-reduce.13.cloned.1.call-done = f32[512,1024]{1,0:T(8,128)} async-done(((f32[512,1024]{1,0:T(8,128)}), f32[512,1024]{1,0:T(8,128)}) %all-reduce.13.cloned.1.call-update) | async-done | bytes 2097168 | tf_op jit(solution)/shard_map/psum | solution.py:35
  367.4 7.6 all_gather.92
  384.9 61.2 %all-reduce.15.cloned.1.call-done = f32[512,1024]{1,0:T(8,128)} async-done(((f32[512,1024]{1,0:T(8,128)}), f32[512,1024]{1,0:T(8,128)}) %all-reduce.15.cloned.1.call-update) | async-done | bytes 2097168 | tf_op jit(solution)/shard_map/psum | solution.py:39
  453.5 8.8 all_gather.95
  486.5 85.6 %all-reduce.17.cloned.1.call-done = f32[512,1024]{1,0:T(8,128)} async-done(((f32[512,1024]{1,0:T(8,128)}), f32[512,1024]{1,0:T(8,128)}) %all-reduce.17.cloned.1.call-update) | async-done | bytes 2097168 | tf_op jit(solution)/shard_map/psum | solution.py:39
  589.3 82.8 %all-reduce.19.cloned.1.call-done = f32[512,1024]{1,0:T(8,128)} async-done(((f32[512,1024]{1,0:T(8,128)}), f32[512,1024]{1,0:T(8,128)}) %all-reduce.19.cloned.1.call-update) | async-done | bytes 2097168 | tf_op jit(solution)/shard_map/psum | solution.py:39
  691.6 10.6 all_gather.97
  717.8 7.0 all_gather.99
  768.9 22.4 %reduce-scatter.17.cloned.1.call-done = f32[128,256]{1,0:T(8,128)} async-done(((f32[1024,256]{1,0:T(8,128)}), f32[128,256]{1,0:T(8,128)}) %reduce-scatter.17.cloned.1.call-update) | async-done | bytes 131088 | tf_op jit(solution)/shard_map/reduce_scatter | solution.py:457
  791.6 192.3 %all-reduce.21.cloned.1.call-done = (f32[512,1024]{1,0:T(8,128)}, f32[512,1024]{1,0:T(8,128)}, f32[256,1024]{1,0:T(8,128)}) async-done(((f32[512,1024]{1,0:T(8,128)}, f32[512,1024]{1,0:T(8,128)}, f32[256,1024]{1,0:T(8,128)}), (f32[512,1024]{1,0:T(8,128)}, f32[512,1024]{1,0:T(8,128)}, f32[256,1024]{1,0:T(8,128)})) %all-reduce.21.cloned.1.call-update) | async-done | bytes 5242896 | tf_op jit(solution)/shard_map/psum | solution.py:35
  990.1 42.5 %reduce-scatter.23.cloned.1.call-done = f32[128,3,256]{2,0,1:T(8,128)} async-done(((f32[1024,3,256]{2,0,1:T(8,128)}), f32[128,3,256]{2,0,1:T(8,128)}) %reduce-scatter.23.cloned.1.call-update) | async-done | bytes 393232 | tf_op jit(solution)/shard_map/reduce_scatter | solution.py:460
  1032.7 45.2 %reduce-scatter.15.cloned.1.call-done = f32[128,2,256]{2,0,1:T(8,128)} async-done(((f32[1024,2,256]{2,0,1:T(8,128)}), f32[128,2,256]{2,0,1:T(8,128)}) %reduce-scatter.15.cloned.1.call-update) | async-done | bytes 262160 | tf_op jit(solution)/shard_map/reduce_scatter | solution.py:456
  1077.9 55.2 %reduce-scatter.27.cloned.1.call-done = f32[128,1024]{1,0:T(8,128)} async-done(((f32[1024,1024]{1,0:T(8,128)}), f32[128,1024]{1,0:T(8,128)}) %reduce-scatter.27.cloned.1.call-update) | async-done | bytes 524304 | tf_op jit(solution)/shard_map/reduce_scatter | solution.py:462
  1133.2 55.4 %reduce-scatter.29.cloned.1.call-done = f32[128,1024]{0,1:T(8,128)} async-done(((f32[1024,1024]{0,1:T(8,128)}), f32[128,1024]{0,1:T(8,128)}) %reduce-scatter.29.cloned.1.call-update) | async-done | bytes 524304 | tf_op jit(solution)/shard_map/reduce_scatter | solution.py:463
  1188.8 55.0 %reduce-scatter.19.cloned.1.call-done = f32[128,1024]{1,0:T(8,128)} async-done(((f32[1024,1024]{1,0:T(8,128)}), f32[128,1024]{1,0:T(8,128)}) %reduce-scatter.19.cloned.1.call-update) | async-done | bytes 524304 | tf_op jit(solution)/shard_map/reduce_scatter | solution.py:458
  1243.9 55.5 %reduce-scatter.21.cloned.1.call-done = f32[128,1024]{1,0:T(8,128)} async-done(((f32[1024,1024]{1,0:T(8,128)}), f32[128,1024]{1,0:T(8,128)}) %reduce-scatter.21.cloned.1.call-update) | async-done | bytes 524304 | tf_op jit(solution)/shard_map/reduce_scatter | solution.py:459
  1299.3 25.2 %all-gather.25.cloned.1.call-done = f32[1024,256]{1,0:T(8,128)} async-done(((f32[128,256]{1,0:T(8,128)}), f32[1024,256]{1,0:T(8,128)}) %all-gather.25.cloned.1.call-update) | async-done | bytes 1048592 | tf_op jit(solution)/shard_map/all_gather | solution.py:484
  1324.5 25.3 %all-gather.13.cloned.1.call-done = f32[1024,256]{1,0:T(8,128)} async-done(((f32[128,256]{1,0:T(8,128)}), f32[1024,256]{1,0:T(8,128)}) %all-gather.13.cloned.1.call-update) | async-done | bytes 1048592 | tf_op jit(solution)/shard_map/all_gather | solution.py:478
  1349.8 25.4 %all-gather.17.cloned.1.call-done = f32[1024,256]{1,0:T(8,128)} async-done(((f32[128,256]{1,0:T(8,128)}), f32[1024,256]{1,0:T(8,128)}) %all-gather.17.cloned.1.call-update) | async-done | bytes 1048592 | tf_op jit(solution)/shard_map/all_gather | solution.py:480
  1382.7 27.3 %reduce-scatter.11.cloned.1.call-done = f32[128,5]{0,1:T(8,128)} async-done(((f32[1024,5]{0,1:T(8,128)}), f32[128,5]{0,1:T(8,128)}) %reduce-scatter.11.cloned.1.call-update) | async-done | bytes 2576 | tf_op jit(solution)/shard_map/reduce_scatter | solution.py:454
  1409.9 12.7 all_gather.101
  1422.7 21.7 %all-gather.23.cloned.1.call-done = f32[1024,3,256]{2,0,1:T(8,128)} async-done(((f32[128,3,256]{2,0,1:T(8,128)}), f32[1024,3,256]{2,0,1:T(8,128)}) %all-gather.23.cloned.1.call-update) | async-done | bytes 3145744 | tf_op jit(solution)/shard_map/all_gather | solution.py:483
  1444.3 30.0 %all-gather.15.cloned.1.call-done = f32[1024,2,256]{2,0,1:T(8,128)} async-done(((f32[128,2,256]{2,0,1:T(8,128)}), f32[1024,2,256]{2,0,1:T(8,128)}) %all-gather.15.cloned.1.call-update) | async-done | bytes 2097168 | tf_op jit(solution)/shard_map/all_gather | solution.py:479
  1478.9 34.3 %all-gather.27.cloned.1.call-done = f32[1024,1024]{1,0:T(8,128)} async-done(((f32[128,1024]{1,0:T(8,128)}), f32[1024,1024]{1,0:T(8,128)}) %all-gather.27.cloned.1.call-update) | async-done | bytes 4194320 | tf_op jit(solution)/shard_map/all_gather | solution.py:485
  1513.1 39.4 %all-gather.29.cloned.1.call-done = f32[1024,1024]{0,1:T(8,128)} async-done(((f32[128,1024]{0,1:T(8,128)}), f32[1024,1024]{0,1:T(8,128)}) %all-gather.29.cloned.1.call-update) | async-done | bytes 4194320 | tf_op jit(solution)/shard_map/all_gather | solution.py:486
  1557.9 33.4 %all-gather.19.cloned.1.call-done = f32[1024,1024]{1,0:T(8,128)} async-done(((f32[128,1024]{1,0:T(8,128)}), f32[1024,1024]{1,0:T(8,128)}) %all-gather.19.cloned.1.call-update) | async-done | bytes 4194320 | tf_op jit(solution)/shard_map/all_gather | solution.py:481
  1591.3 38.6 %all-gather.21.cloned.1.call-done = f32[1024,1024]{1,0:T(8,128)} async-done(((f32[128,1024]{1,0:T(8,128)}), f32[1024,1024]{1,0:T(8,128)}) %all-gather.21.cloned.1.call-update) | async-done | bytes 4194320 | tf_op jit(solution)/shard_map/all_gather | solution.py:482
  (444 shorter events, 262.1 us)
Async XLA Ops:
  7.2 345.3 %copy-start = (bf16[1024,1024]{1,0:T(8,128)(2,1)S(1)}, bf16[1024,1024]{1,0:T(8,128)(2,1)}, u32[]{:S(2)}) copy-start(bf16[1024,1024]{1,0:T(8,128)(2,1)} %param.31) | copy-start | bytes 6291460
  7.2 123.2 %all-reduce.9.cloned.1.call-start = ((), (), s32[]{:S(2)}) async-start(), calls=%async_computation.10 | async-start | bytes 4194304 | tf_op jit(solution)/shard_map/psum | solution.py:35
  42.3 183.4 %all-reduce.11.cloned.1.call-start = ((), (), s32[]{:S(2)}) async-start(), calls=%async_computation.11 | async-start | bytes 4194304 | tf_op jit(solution)/shard_map/psum | solution.py:35
  140.1 208.6 %all-reduce.13.cloned.1.call-start = ((), (), s32[]{:S(2)}) async-start(), calls=%async_computation.12 | async-start | bytes 4194304 | tf_op jit(solution)/shard_map/psum | solution.py:35
  262.7 183.4 %all-reduce.15.cloned.1.call-start = ((), (), s32[]{:S(2)}) async-start(), calls=%async_computation.13 | async-start | bytes 4194304 | tf_op jit(solution)/shard_map/psum | solution.py:39
  360.4 211.7 %all-reduce.17.cloned.1.call-start = ((), (), s32[]{:S(2)}) async-start(), calls=%async_computation.14 | async-start | bytes 4194304 | tf_op jit(solution)/shard_map/psum | solution.py:39
  486.3 185.8 %all-reduce.19.cloned.1.call-start = ((), (), s32[]{:S(2)}) async-start(), calls=%async_computation.15 | async-start | bytes 4194304 | tf_op jit(solution)/shard_map/psum | solution.py:39
  586.5 181.3 %reduce-scatter.25.cloned.1.call-start = ((), (), s32[]{:S(2)}) async-start(), calls=%async_computation.29 | async-start | bytes 1179648 | tf_op jit(solution)/shard_map/reduce_scatter | solution.py:461
  589.3 86.5 %copy-start.80 = (f32[512]{0:T(512)S(1)}, f32[512]{0:T(512)}, u32[]{:S(2)}) copy-start(f32[512]{0:T(512)} %copy-done.79) | copy-start | bytes 6148
  589.3 179.1 %reduce-scatter.13.cloned.1.call-start = ((), (), s32[]{:S(2)}) async-start(), calls=%async_computation.17 | async-start | bytes 1179648 | tf_op jit(solution)/shard_map/reduce_scatter | solution.py:455
  686.2 105.1 %reduce-scatter.17.cloned.1.call-start = ((), (), s32[]{:S(2)}) async-start(), calls=%async_computation.21 | async-start | bytes 1179648 | tf_op jit(solution)/shard_map/reduce_scatter | solution.py:457
  707.8 276.1 %all-reduce.21.cloned.1.call-start = ((), (), s32[]{:S(2)}) async-start(), calls=%async_computation.35 | async-start | bytes 10485760 | tf_op jit(solution)/shard_map/psum | solution.py:35
  733.1 299.5 %reduce-scatter.23.cloned.1.call-start = ((), (), s32[]{:S(2)}) async-start(), calls=%async_computation.27 | async-start | bytes 3538944 | tf_op jit(solution)/shard_map/reduce_scatter | solution.py:460
  741.9 336.0 %reduce-scatter.15.cloned.1.call-start = ((), (), s32[]{:S(2)}) async-start(), calls=%async_computation.19 | async-start | bytes 2359296 | tf_op jit(solution)/shard_map/reduce_scatter | solution.py:456
  745.6 387.6 %reduce-scatter.27.cloned.1.call-start = ((), (), s32[]{:S(2)}) async-start(), calls=%async_computation.31 | async-start | bytes 4718592 | tf_op jit(solution)/shard_map/reduce_scatter | solution.py:462
  750.4 438.3 %reduce-scatter.29.cloned.1.call-start = ((), (), s32[]{:S(2)}) async-start(), calls=%async_computation.33 | async-start | bytes 4718592 | tf_op jit(solution)/shard_map/reduce_scatter | solution.py:463
  755.8 488.0 %reduce-scatter.19.cloned.1.call-start = ((), (), s32[]{:S(2)}) async-start(), calls=%async_computation.23 | async-start | bytes 4718592 | tf_op jit(solution)/shard_map/reduce_scatter | solution.py:458
  761.8 537.5 %reduce-scatter.21.cloned.1.call-start = ((), (), s32[]{:S(2)}) async-start(), calls=%async_computation.25 | async-start | bytes 4718592 | tf_op jit(solution)/shard_map/reduce_scatter | solution.py:459
  767.6 218.2 %copy-start.115 = (f32[256]{0:T(256)S(1)}, f32[256]{0:T(256)}, u32[]{:S(2)}) copy-start(f32[256]{0:T(256)} %copy-done.114) | copy-start | bytes 3076
  767.6 220.1 %copy-start.73 = (f32[1,1024]{1,0:T(1,128)S(1)}, f32[1,1024]{1,0:T(1,128)}, u32[]{:S(2)}) copy-start(f32[1,1024]{1,0:T(1,128)} %copy-done.72) | copy-start | bytes 12292
  767.7 220.1 %copy-start.78 = (f32[512]{0:T(512)S(1)}, f32[512]{0:T(512)}, u32[]{:S(2)}) copy-start(f32[512]{0:T(512)} %copy-done.77) | copy-start | bytes 6148
  767.7 556.9 %all-gather.25.cloned.1.call-start = ((), (), s32[]{:S(2)}) async-start(), calls=%async_computation.30 | async-start | bytes 1179648 | tf_op jit(solution)/shard_map/all_gather | solution.py:484
  768.3 581.5 %all-gather.13.cloned.1.call-start = ((), (), s32[]{:S(2)}) async-start(), calls=%async_computation.18 | async-start | bytes 1179648 | tf_op jit(solution)/shard_map/all_gather | solution.py:478
  768.8 606.4 %all-gather.17.cloned.1.call-start = ((), (), s32[]{:S(2)}) async-start(), calls=%async_computation.22 | async-start | bytes 1179648 | tf_op jit(solution)/shard_map/all_gather | solution.py:480
  791.3 618.6 %reduce-scatter.11.cloned.1.call-start = ((), (), s32[]{:S(2)}) async-start(), calls=%async_computation.16 | async-start | bytes 36864 | tf_op jit(solution)/shard_map/reduce_scatter | solution.py:454
  990.1 454.3 %all-gather.23.cloned.1.call-start = ((), (), s32[]{:S(2)}) async-start(), calls=%async_computation.28 | async-start | bytes 3538944 | tf_op jit(solution)/shard_map/all_gather | solution.py:483
  1032.6 441.7 %all-gather.15.cloned.1.call-start = ((), (), s32[]{:S(2)}) async-start(), calls=%async_computation.20 | async-start | bytes 2359296 | tf_op jit(solution)/shard_map/all_gather | solution.py:479
  1077.9 435.2 %all-gather.27.cloned.1.call-start = ((), (), s32[]{:S(2)}) async-start(), calls=%async_computation.32 | async-start | bytes 4718592 | tf_op jit(solution)/shard_map/all_gather | solution.py:485
  1133.2 419.3 %all-gather.29.cloned.1.call-start = ((), (), s32[]{:S(2)}) async-start(), calls=%async_computation.34 | async-start | bytes 4718592 | tf_op jit(solution)/shard_map/all_gather | solution.py:486
  1188.7 402.6 %all-gather.19.cloned.1.call-start = ((), (), s32[]{:S(2)}) async-start(), calls=%async_computation.24 | async-start | bytes 4718592 | tf_op jit(solution)/shard_map/all_gather | solution.py:481
  1243.8 386.1 %all-gather.21.cloned.1.call-start = ((), (), s32[]{:S(2)}) async-start(), calls=%async_computation.26 | async-start | bytes 4718592 | tf_op jit(solution)/shard_map/all_gather | solution.py:482
  1478.8 151.7 %copy-start.55 = (f32[1024,256]{1,0:T(8,128)S(1)}, f32[1024,256]{1,0:T(8,128)}, u32[]{:S(2)}) copy-start(f32[1024,256]{1,0:T(8,128)} %all-gather.13.cloned.1.call-done) | copy-start | bytes 3145732
  (123 other events, 616.5 us)
Sparse Core Ops, SparseCore 0:
  42.4 87.9 all-reduce.8
  140.2 85.4 all-reduce.10
  262.8 85.9 all-reduce.12
  360.6 85.4 all-reduce.14
  486.4 85.6 all-reduce.16
  586.6 85.4 all-reduce.18
  675.3 36.3 reduce-scatter.24
  715.4 36.0 reduce-scatter.12
  755.3 35.9 reduce-scatter.16
  794.3 189.5 all-reduce.20
  987.3 45.2 reduce-scatter.22
  1036.6 41.1 reduce-scatter.14
  1081.8 51.3 reduce-scatter.26
  1137.3 51.3 reduce-scatter.28
  1192.5 51.2 reduce-scatter.18
  1247.9 51.3 reduce-scatter.20
  1301.0 23.4 all-gather.24
  1326.3 23.4 all-gather.12
  1351.7 23.4 all-gather.16
  1378.6 31.2 reduce-scatter.10
  1412.0 32.2 all-gather.22
  1446.4 27.8 all-gather.14
  1476.4 36.7 all-gather.26
  1515.0 37.4 all-gather.28
  1554.5 36.7 all-gather.18
  1593.2 36.7 all-gather.20
where the time goes:
time: 1660 us; the launch traced here: 1650 us
  waiting for transfers between devices  1310 us (79%)
  blocking collectives  108 us (7%)
  matrix products  107 us (6%)
  local copies, waits for them, and re-layouts  68.7 us (4%)
  other arithmetic  46.2 us (3%)
    psum x4, waiting for transfers between devices, head_sum(): return lax.psum(partial_sum, 'head')  444 us
    psum x3, waiting for transfers between devices, head_grad_sum(): return lax.psum(partial_sum, 'head')  230 us
    unnamed x272, local copies, waits for them, and re-layouts  56.4 us
    reduce_scatter x1, waiting for transfers between devices, per_device(): lax.psum_scatter(grad_out_a, ('group', 'blk'), scatter_dimension=0, tiled...  55.5 us
    reduce_scatter x1, waiting for transfers between devices, per_device(): lax.psum_scatter(grad_out_b, ('group', 'blk'), scatter_dimension=0, tiled...  55.4 us
    reduce_scatter x1, waiting for transfers between devices, per_device(): lax.psum_scatter(grad_in_b, ('group', 'blk'), scatter_dimension=0, tiled=...  55.2 us
    reduce_scatter x1, waiting for transfers between devices, per_device(): lax.psum_scatter(grad_in_a, ('group', 'blk'), scatter_dimension=0, tiled=...  55 us
    reduce_scatter x1, waiting for transfers between devices, per_device(): lax.psum_scatter(grad_kv_cross, ('group', 'blk'), scatter_dimension=0, ti...  45.2 us
  transfers between devices with their start and end apart: 26, of which 24 were waited for; matrix products, arithmetic and copies ran while one was open for 6% of the time, Pallas kernels for 0%

commit v1 on v0

--- a/solution.py
+++ b/solution.py
@@ -1,6 +1,11 @@
+import functools
+import types
+
 import jax
 import jax.numpy as jnp
 from jax import lax
+from jax.experimental import pallas as pl
+from jax.experimental.pallas import tpu as pltpu
 from jax.sharding import PartitionSpec as P
 
 HEAD_DIM = 128
@@ -502,9 +507,888 @@
     )
 
 
+MESH = pl.DeviceIdType.MESH
+bf16, f32 = jnp.bfloat16, jnp.float32
+LANES = 128
+SCALE = HEAD_DIM**-0.5
+GELU_A = 0.7978845608028654
+GELU_B = 0.044715
+
+
+def dot_nn(a, b):
+    return jnp.dot(a, b, preferred_element_type=f32)
+
+
+def dot_nt(a, b):
+    return lax.dot_general(a, b, (((1,), (1,)), ((), ())), preferred_element_type=f32)
+
+
+def dot_tn(a, b):
+    return lax.dot_general(a, b, (((0,), (0,)), ((), ())), preferred_element_type=f32)
+
+
+def norm_rows(x):
+    c = x - jnp.mean(x, axis=-1, keepdims=True)
+    rstd = lax.rsqrt(jnp.mean(c * c, axis=-1, keepdims=True) + 1e-05)
+    return c * rstd, rstd
+
+
+def gelu_both(u):
+    u2 = u * u
+    t = jnp.tanh(GELU_A * u * (1.0 + GELU_B * u2))
+    half = 0.5 * (1.0 + t)
+    slope = half + 0.5 * u * (1.0 - t * t) * (GELU_A * (1.0 + 3.0 * GELU_B * u2))
+    return u * half, slope
+
+
+def loop(start, stop, body):
+    def step(k, carry):
+        body(k)
+        return carry
+
+    lax.fori_loop(start, stop, step, 0)
+
+
+def block_kernel(names, T, I, D, C, F, CH, *refs):
+    r = types.SimpleNamespace(**dict(zip(names, refs, strict=True)))
+    NCH = T // CH
+    ICH = I // CH
+    HL = C // HEAD_DIM
+    g = lax.axis_index("group")
+    b = lax.axis_index("blk")
+    h = lax.axis_index("head")
+    is_mid = (h == 1) | (h == 2)
+    is_end = jnp.logical_not(is_mid)
+    at_pair = (g, b, h ^ 1)
+    at_mid = (g, b, 3 - h)
+    at_y = (g, 1 - b, h)
+    at_x = (g ^ 2, b, h)
+    at_core = (g ^ 1, b, h)
+    core = g % 2
+    xi = g // 2
+    gains = r.gains
+
+    def rows(c, n=CH):
+        return pl.ds(pl.multiple_of(c * n, n), n)
+
+    def remote(src, dst, send_sem, recv_sem, where):
+        return pltpu.make_async_remote_copy(
+            src_ref=src, dst_ref=dst, send_sem=send_sem, recv_sem=recv_sem, device_id=where, device_id_type=MESH
+        )
+
+    bar = pltpu.get_barrier_semaphore()
+    for where in (at_pair, at_y, at_x, at_core):
+        pl.semaphore_signal(bar, inc=1, device_id=where, device_id_type=MESH)
+
+    @pl.when(is_mid)
+    def _():
+        pl.semaphore_signal(bar, inc=1, device_id=at_mid, device_id_type=MESH)
+
+    loads = {}
+
+    def load(src, dst, name):
+        cp = pltpu.make_async_copy(src, dst, r.load_sem.at[len(loads)])
+        cp.start()
+        loads[name] = cp
+
+    load(r.inputs, r.inp, "inp")
+    load(r.w_kv_c, r.wkvc, "wkvc")
+    load(r.latents, r.lat, "lat")
+    load(r.w_q_c, r.wqc, "wqc")
+    load(r.w_o_c, r.woc, "woc")
+    load(r.w_in_a, r.wina, "wina")
+    load(r.w_out_a, r.wouta, "wouta")
+    load(r.w_qkv_s, r.wqkvs, "wqkvs")
+    load(r.w_o_s, r.wos, "wos")
+    load(r.w_in_b, r.winb, "winb")
+    load(r.w_out_b, r.woutb, "woutb")
+    load(r.out_grad, r.r4, "r4")
+
+    lg = r.latent_group[...]
+    ic = jnp.where(r.input_valid[...] == 1, r.input_group[...], -1).astype(f32)
+    sc = jnp.where(r.latent_valid[...] == 1, lg, -1).astype(f32)
+    lgf = lg.astype(f32)
+    r.codes[:, 0:I] = jnp.broadcast_to(ic, (8, I))
+    r.codes[:, I : I + T] = jnp.broadcast_to(sc, (8, T))
+    r.codes[:, I + T : I + 2 * T] = jnp.broadcast_to(lgf, (8, T))
+
+    def make_columns(line, dst):
+        for j in range(T // LANES):
+            dst[pl.ds(j * LANES, LANES), :] = jnp.transpose(
+                jnp.broadcast_to(line[:, j * LANES : (j + 1) * LANES], (LANES, LANES))
+            )
+
+    make_columns(lgf, r.qcol)
+    r.dg[...] = jnp.zeros_like(r.dg)
+
+    @pl.when(is_mid)
+    def _():
+        pl.semaphore_wait(bar, 5)
+
+    @pl.when(is_end)
+    def _():
+        pl.semaphore_wait(bar, 4)
+
+    def to_y(src, dst, k):
+        return remote(src, dst, r.y_snd.at[k], r.y_rcv.at[k], at_y)
+
+    codes_cp = to_y(r.codes, r.codes_o, 0)
+    codes_cp.start()
+
+    def cp_in(p, c):
+        return remote(r.part.at[p, rows(c)], r.rin.at[p, rows(c)], r.ar_snd.at[p, c], r.ar_in.at[p, c], at_pair)
+
+    def cp_mid(p, c):
+        return remote(r.part.at[p, rows(c)], r.rmid.at[p, rows(c)], r.ar_snd.at[p, c], r.ar_mid.at[p, c], at_mid)
+
+    def cp_tot(p, c):
+        return remote(r.rin.at[p, rows(c)], r.rin.at[p, rows(c)], r.ar_tot.at[p, c], r.ar_in.at[p, c], at_pair)
+
+    def ar_send(p, c):
+        @pl.when(is_end)
+        def _():
+            cp_in(p, c).start()
+
+    def ar_put(p, c, value):
+        r.part[p, rows(c)] = value.astype(bf16)
+        ar_send(p, c)
+
+    def ar_b(p, c):
+        @pl.when(is_mid)
+        def _():
+            cp_in(p, c).wait_recv()
+            total = r.part[p, rows(c)].astype(f32) + r.rin[p, rows(c)].astype(f32)
+            r.part[p, rows(c)] = total.astype(bf16)
+            cp_mid(p, c).start()
+
+    def ar_c(p, c, prev=None):
+        @pl.when(is_mid)
+        def _():
+            cp_mid(p, c).wait_recv()
+            cp_mid(p, c).wait_send()
+            total = r.part[p, rows(c)].astype(f32) + r.rmid[p, rows(c)].astype(f32)
+            r.rin[p, rows(c)] = total.astype(bf16)
+            if prev is not None:
+                cp_tot(prev, c).wait_send()
+            cp_tot(p, c).start()
+
+        @pl.when(is_end)
+        def _():
+            cp_in(p, c).wait_send()
+            cp_tot(p, c).wait_recv()
+
+    def total_of(p, c):
+        return r.rin[p, rows(c)].astype(f32)
+
+    half, quarter, eighth, piece = D // 2, D // 4, D // 8, D // 16
+    own = core * half
+    p_own = own + xi * eighth
+    p_oth = own + (1 - xi) * eighth
+    q_base = own + quarter
+    q_own = q_base + b * eighth
+    q_oth = q_base + (1 - b) * eighth
+    p_fin, p_fin_oth = p_own + b * piece, p_own + (1 - b) * piece
+    q_fin, q_fin_oth = q_own + xi * piece, q_own + (1 - xi) * piece
+
+    def span(start, n):
+        return pl.ds(pl.multiple_of(start, piece), n)
+
+    class Job:
+        def __init__(self, index, w, slot, out, parts):
+            self.j, self.w, self.s, self.out, self.parts = index, w, slot, out, parts
+
+        def tile(self, t):
+            col = 0
+            rw = rows(t, LANES)
+            for lhs, rhs in self.parts:
+                n = rhs.shape[1]
+                self.w[rw, col : col + n] = dot_tn(lhs[:, rw], rhs[...]).astype(bf16)
+                col += n
+
+        def cp(self, k, src, dst, where):
+            return remote(src, dst, r.j_snd.at[self.j, k], r.j_rcv.at[self.j, k], where)
+
+        def cp_core(self):
+            return self.cp(0, self.w.at[span((1 - core) * half, half)], r.rc.at[self.s], at_core)
+
+        def cp_p1(self):
+            return self.cp(1, self.w.at[span(p_oth, eighth)], r.r1p.at[self.s], at_x)
+
+        def cp_q1(self):
+            return self.cp(2, self.w.at[span(q_oth, eighth)], r.r1q.at[self.s], at_y)
+
+        def cp_p2(self):
+            return self.cp(3, self.w.at[span(p_fin_oth, piece)], r.r2p.at[self.s], at_y)
+
+        def cp_q2(self):
+            return self.cp(4, self.w.at[span(q_fin_oth, piece)], r.r2q.at[self.s], at_x)
+
+        def cp_p3(self):
+            return self.cp(5, self.w.at[span(p_fin, piece)], self.out.at[span(p_fin, piece)], at_y)
+
+        def cp_q3(self):
+            return self.cp(6, self.w.at[span(q_fin, piece)], self.out.at[span(q_fin, piece)], at_x)
+
+        def cp_p4(self):
+            return self.cp(7, self.out.at[span(p_own, eighth)], self.out.at[span(p_own, eighth)], at_x)
+
+        def cp_q4(self):
+            return self.cp(8, self.out.at[span(q_own, eighth)], self.out.at[span(q_own, eighth)], at_y)
+
+        def cp_all(self):
+            return self.cp(9, self.out.at[span(own, half)], self.out.at[span(own, half)], at_core)
+
+        def cp_keep(self):
+            return (
+                pltpu.make_async_copy(
+                    self.w.at[span(p_fin, piece)], self.out.at[span(p_fin, piece)], r.j_own.at[self.j, 0]
+                ),
+                pltpu.make_async_copy(
+                    self.w.at[span(q_fin, piece)], self.out.at[span(q_fin, piece)], r.j_own.at[self.j, 1]
+                ),
+            )
+
+        def add(self, start, n, other):
+            rw = span(start, n)
+            self.w[rw] = (self.w[rw].astype(f32) + other[...].astype(f32)).astype(bf16)
+
+        def start(self):
+            self.cp_core().start()
+
+        def s1(self):
+            self.cp_core().wait_recv()
+            self.add(p_oth, eighth, r.rc.at[self.s, span(p_oth - own, eighth)])
+            self.cp_p1().start()
+            self.add(q_oth, eighth, r.rc.at[self.s, span(q_oth - own, eighth)])
+            self.cp_q1().start()
+            self.add(p_own, eighth, r.rc.at[self.s, span(p_own - own, eighth)])
+            self.add(q_own, eighth, r.rc.at[self.s, span(q_own - own, eighth)])
+
+        def s2(self):
+            self.cp_p1().wait_recv()
+            self.add(p_own, eighth, r.r1p.at[self.s])
+            self.cp_p2().start()
+            self.cp_q1().wait_recv()
+            self.add(q_own, eighth, r.r1q.at[self.s])
+            self.cp_q2().start()
+
+        def s3(self):
+            self.cp_p2().wait_recv()
+            self.add(p_fin, piece, r.r2p.at[self.s])
+            self.cp_p3().start()
+            self.cp_q2().wait_recv()
+            self.add(q_fin, piece, r.r2q.at[self.s])
+            self.cp_q3().start()
+            for cp in self.cp_keep():
+                cp.start()
+
+        def s4(self):
+            for cp in self.cp_keep():
+                cp.wait()
+            self.cp_p3().wait_recv()
+            self.cp_p4().start()
+            self.cp_q3().wait_recv()
+            self.cp_q4().start()
+            for cp in (self.cp_core(), self.cp_p1(), self.cp_q1(), self.cp_p2(), self.cp_q2(), self.cp_p3(), self.cp_q3()):
+                cp.wait_send()
+
+        def s5(self):
+            self.cp_p4().wait_recv()
+            self.cp_q4().wait_recv()
+            self.cp_all().start()
+            self.cp_p4().wait_send()
+            self.cp_q4().wait_send()
+
+        def s6(self):
+            self.cp_all().wait()
+
+    job_out_b = Job(0, r.woutb, 0, r.g_out_b, [(r.r4, r.z2)])
+    job_in_b = Job(1, r.winb, 1, r.g_in_b, [(r.h2, r.du2)])
+    job_self = Job(2, r.wj, 2, r.g_self, [(r.cs, r.dqkv), (r.ra, r.o_s)])
+    job_out_a = Job(3, r.woutb, 0, r.g_out_a, [(r.rb, r.z1)])
+    job_in_a = Job(4, r.winb, 1, r.g_in_a, [(r.h1, r.du1)])
+    job_cross = Job(5, r.wj, 2, r.g_cross, [(r.bn, r.dkv), (r.an, r.dq), (r.ra, r.o_c)])
+
+    def norm_out(x, gain_row, out, rstd_out, rw):
+        xhat, rstd = norm_rows(x)
+        rstd_out[rw] = jnp.broadcast_to(rstd, (rstd.shape[0], LANES))
+        low = (xhat * gains[gain_row : gain_row + 1, :]).astype(bf16)
+        out[rw] = low
+        return low
+
+    def norm_grad(cot, low_ref, gain_row, rstd_ref, rw):
+        gain = gains[gain_row : gain_row + 1, :]
+        xhat = low_ref[rw].astype(f32) * (1.0 / gain)
+        scaled = cot * gain
+        mean_one = jnp.mean(scaled, axis=-1, keepdims=True)
+        mean_two = jnp.mean(scaled * xhat, axis=-1, keepdims=True)
+        r.dg[gain_row : gain_row + 1, :] += jnp.sum(cot * xhat, axis=0, keepdims=True)
+        return rstd_ref[rw, 0:1] * (scaled - mean_one - xhat * mean_two)
+
+    loads["inp"].wait()
+    loads["wkvc"].wait()
+
+    def kv_chunk(k):
+        rw = rows(k, LANES)
+        low = norm_out(r.inp[rw].astype(f32), 1, r.bn, r.rs1, rw)
+        r.kv[rw] = dot_nn(low, r.wkvc[...]).astype(bf16)
+
+    loop(0, I // LANES, kv_chunk)
+    kv_cp = to_y(r.kv.at[pl.ds(0, I)], r.kv.at[pl.ds(I, I)], 1)
+    kv_cp.start()
+    loads["lat"].wait()
+    loads["wqc"].wait()
+
+    def q_chunk(k):
+        rw = rows(k, LANES)
+        low = norm_out(r.lat[rw].astype(f32), 0, r.an, r.rs0, rw)
+        r.q[rw] = dot_nn(low, r.wqc[...]).astype(bf16)
+
+    loop(0, T // LANES, q_chunk)
+    codes_cp.wait()
+    make_columns(r.codes_o[0:1, I + T : I + 2 * T], r.qcol_o)
+    kv_cp.wait()
+    loads["woc"].wait()
+
+    def attend_chunk(k, q_ref, kv_ref, p_ref, o_ref, start, n):
+        rw = rows(k)
+        kc = jnp.concatenate([r.codes[0:1, start : start + n], r.codes_o[0:1, start : start + n]], axis=1)
+        allowed = r.qcol[rw, 0:1] == kc
+        for hd in range(HL):
+            cols = slice(hd * HEAD_DIM, (hd + 1) * HEAD_DIM)
+            vcols = slice(C + hd * HEAD_DIM, C + (hd + 1) * HEAD_DIM)
+            s = jnp.where(allowed, dot_nt(q_ref[rw, cols], kv_ref[:, cols]) * SCALE, masked_fill)
+            e = jnp.exp(s - jnp.max(s, axis=-1, keepdims=True))
+            p = (e * (1.0 / jnp.sum(e, axis=-1, keepdims=True))).astype(bf16)
+            p_ref[hd, rw, :] = p
+            o_ref[rw, cols] = dot_nn(p, kv_ref[:, vcols]).astype(bf16)
+
+    def cross_chunk(k):
+        attend_chunk(k, r.q, r.kv, r.p_c, r.o_c, 0, I)
+        ar_put(0, k, dot_nt(r.o_c[rows(k)], r.woc[...]))
+
+        @pl.when(k >= 4)
+        def _():
+            ar_b(0, k - 4)
+
+    loop(0, NCH, cross_chunk)
+    back_cross = [
+        to_y(r.p_c.at[:, :, pl.ds(I, I)], r.pr_c, 2), to_y(r.q, r.qr_c, 3), to_y(r.o_c, r.or_c, 4),
+    ]
+    for cp in back_cross:
+        cp.start()
+    loads["wina"].wait()
+    loads["wouta"].wait()
+
+    def first_chunk(m):
+        @pl.when((m >= 2) & (m < NCH - 2))
+        def _():
+            ar_b(0, m + 2)
+
+        ar_c(0, m)
+        rw = rows(m)
+        x = r.lat[rw].astype(f32) + total_of(0, m)
+        r.xs[rw] = x
+        low = norm_out(x, 2, r.h1, r.rs2, rw)
+        z, slope = gelu_both(dot_nn(low, r.wina[...]))
+        z = z.astype(bf16)
+        r.z1[rw] = z
+        r.s1[rw] = slope.astype(bf16)
+        ar_put(1, m, dot_nt(z, r.wouta[...]))
+
+        @pl.when(m >= NCH - 2)
+        def _():
+            ar_b(1, m + 2 - NCH)
+
+    loop(0, NCH, first_chunk)
+    loads["wqkvs"].wait()
+    loads["wos"].wait()
+
+    def kv2_cp(c):
+        return remote(r.kv2.at[rows(c)], r.kv2.at[rows(c + NCH)], r.kv_snd.at[c], r.kv_rcv.at[c], at_y)
+
+    def second_chunk(m):
+        @pl.when(m < NCH - 2)
+        def _():
+            ar_b(1, m + 2)
+
+        ar_c(1, m, 0)
+        rw = rows(m)
+        x = r.xs[rw] + total_of(1, m)
+        r.xs[rw] = x
+        low = norm_out(x, 3, r.cs, r.rs3, rw)
+        qkv = dot_nn(low, r.wqkvs[...]).astype(bf16)
+        r.q2[rw] = qkv[:, :C]
+        r.kv2[rw] = qkv[:, C:]
+        kv2_cp(m).start()
+
+    loop(0, NCH, second_chunk)
+    loop(0, NCH, lambda c: kv2_cp(c).wait())
+
+    def self_chunk(k):
+        attend_chunk(k, r.q2, r.kv2, r.p_s, r.o_s, I, T)
+        ar_put(0, k, dot_nt(r.o_s[rows(k)], r.wos[...]))
+
+        @pl.when(k >= 4)
+        def _():
+            ar_b(0, k - 4)
+
+    loop(0, NCH, self_chunk)
+    back_self = [
+        to_y(r.p_s.at[:, :, pl.ds(T, T)], r.pr_s, 5), to_y(r.q2, r.qr_s, 6), to_y(r.o_s, r.or_s, 7),
+    ]
+    for cp in back_self:
+        cp.start()
+    loads["winb"].wait()
+    loads["woutb"].wait()
+    loads["r4"].wait()
+
+    def third_chunk(m):
+        @pl.when((m >= 2) & (m < NCH - 2))
+        def _():
+            ar_b(0, m + 2)
+
+        ar_c(0, m, 1)
+        rw = rows(m)
+        x = r.xs[rw] + total_of(0, m)
+        r.xs[rw] = x
+        low = norm_out(x, 4, r.h2, r.rs4, rw)
+        z, slope = gelu_both(dot_nn(low, r.winb[...]))
+        z = z.astype(bf16)
+        r.z2[rw] = z
+        du = (dot_nn(r.r4[rw], r.woutb[...]) * slope).astype(bf16)
+        r.du2[rw] = du
+        ar_put(1, m, dot_nt(du, r.winb[...]))
+        r.part[2, rw] = dot_nt(z, r.woutb[...]).astype(bf16)
+
+        @pl.when(m >= NCH - 2)
+        def _():
+            ar_b(1, m + 2 - NCH)
+
+    loop(0, NCH, third_chunk)
+
+    def d_o_cp(k, c):
+        return remote(r.do.at[k, rows(c)], r.do_o.at[k, rows(c)], r.do_snd.at[k, c], r.do_rcv.at[k, c], at_y)
+
+    def fifth_chunk(m):
+        @pl.when(m < NCH - 2)
+        def _():
+            ar_b(1, m + 2)
+
+        ar_c(1, m, 0)
+        rw = rows(m)
+        dx = r.r4[rw].astype(f32) + norm_grad(total_of(1, m), r.h2, 4, r.rs4, rw)
+        r.dxs[rw] = dx
+        low = dx.astype(bf16)
+        r.ra[rw] = low
+        r.do[0, rw] = dot_nn(low, r.wos[...]).astype(bf16)
+        d_o_cp(0, m).start()
+
+        @pl.when(m < NCH // 2)
+        def _():
+            job_out_b.tile(2 * m)
+            job_out_b.tile(2 * m + 1)
+
+        @pl.when(m == NCH // 2)
+        def _():
+            job_out_b.start()
+
+        @pl.when(m >= NCH // 2)
+        def _():
+            job_in_b.tile(2 * m - NCH)
+            job_in_b.tile(2 * m + 1 - NCH)
+
+    loop(0, NCH, fifth_chunk)
+    job_in_b.start()
+
+    def late_sends(lo, hi):
+        loop(lo, hi, lambda c: ar_send(2, c))
+
+    def late_out(c):
+        ar_c(2, c)
+        rw = rows(c)
+        r.part[2, rw] = (r.xs[rw] + total_of(2, c)).astype(bf16)
+
+    late_sends(0, NCH // 2)
+
+    QB = 128
+
+    def attend_back(hd, do, do_o, q_ref, qr_ref, kv_ref, p_ref, pr_ref, o_ref, or_ref, n, start, dq_ref, dq_col, dkv_ref, dkv_col, between, waits):
+        cols = slice(hd * HEAD_DIM, (hd + 1) * HEAD_DIM)
+        vcols = slice(C + hd * HEAD_DIM, C + (hd + 1) * HEAD_DIM)
+
+        def own_queries(k):
+            rw = rows(k, QB)
+            grad = do[rw, cols]
+            delta = jnp.sum(grad.astype(f32) * o_ref[rw, cols].astype(f32), axis=-1, keepdims=True)
+            kc = jnp.concatenate([r.codes[0:1, start : start + n], r.codes_o[0:1, start : start + n]], axis=1)
+            diff = dot_nt(grad, kv_ref[:, vcols]) - delta
+            ds = jnp.where(r.qcol[rw, 0:1] == kc, p_ref[hd, rw, :].astype(f32) * diff, 0.0).astype(bf16)
+            r.ds[rw, 0:n] = ds[:, 0:n]
+            dq_ref[rw, dq_col + hd * HEAD_DIM : dq_col + (hd + 1) * HEAD_DIM] = (
+                dot_nn(ds, kv_ref[:, cols]) * SCALE
+            ).astype(bf16)
+
+        loop(0, T // QB, own_queries)
+        between()
+        for wait in waits:
+            wait()
+
+        def other_queries(k):
+            rw = rows(k, QB)
+            grad = do_o[rw, cols]
+            delta = jnp.sum(grad.astype(f32) * or_ref[rw, cols].astype(f32), axis=-1, keepdims=True)
+            diff = dot_nt(grad, kv_ref[0:n, vcols]) - delta
+            allowed = r.qcol_o[rw, 0:1] == r.codes[0:1, start : start + n]
+            ds = jnp.where(allowed, pr_ref[hd, rw, :].astype(f32) * diff, 0.0).astype(bf16)
+            r.ds[rows(k + T // QB, QB), 0:n] = ds
+
+        loop(0, T // QB, other_queries)
+        dk = dot_tn(r.ds[0:T, 0:n], q_ref[:, cols]) + dot_tn(r.ds[T : 2 * T, 0:n], qr_ref[:, cols])
+        dkv_ref[:, dkv_col + hd * HEAD_DIM : dkv_col + (hd + 1) * HEAD_DIM] = (dk * SCALE).astype(bf16)
+        dv = dot_tn(p_ref[hd, :, 0:n], do[:, cols]) + dot_tn(pr_ref[hd], do_o[:, cols])
+        dkv_ref[:, dkv_col + C + hd * HEAD_DIM : dkv_col + C + (hd + 1) * HEAD_DIM] = dv.astype(bf16)
+
+    def wait_d_o(k):
+        loop(0, NCH, lambda c: d_o_cp(k, c).wait())
+
+    for hd in range(HL):
+        waits = [] if hd else [functools.partial(wait_d_o, 0)] + [cp.wait for cp in back_self]
+        attend_back(
+            hd, r.do.at[0], r.do_o.at[0], r.q2, r.qr_s, r.kv2, r.p_s, r.pr_s, r.o_s, r.or_s, T, I, r.dqkv, 0, r.dqkv, C,
+            (lambda: None) if hd else job_out_b.s1, waits,
+        )
+        if hd == 0:
+            ar_b(2, 0)
+            ar_b(2, 1)
+            job_in_b.s1()
+
+    def sixth_put(k):
+        ar_put(0, k, dot_nt(r.dqkv[rows(k)], r.wqkvs[...]))
+
+    loop(0, NCH, sixth_put)
+    job_out_b.s2()
+    loop(2, NCH // 2, lambda c: ar_b(2, c))
+    job_in_b.s2()
+    loop(0, 2, lambda c: ar_b(0, c))
+
+    def sixth_chunk(m):
+        @pl.when(m < NCH - 2)
+        def _():
+            ar_b(0, m + 2)
+
+        ar_c(0, m, 1)
+        rw = rows(m)
+        dx = r.dxs[rw] + norm_grad(total_of(0, m), r.cs, 3, r.rs3, rw)
+        r.dxs[rw] = dx
+        low = dx.astype(bf16)
+        r.rb[rw] = low
+        du = (dot_nn(low, r.wouta[...]) * r.s1[rw].astype(f32)).astype(bf16)
+        r.du1[rw] = du
+        ar_put(1, m, dot_nt(du, r.wina[...]))
+
+        @pl.when(m >= NCH - 2)
+        def _():
+            ar_b(1, m + 2 - NCH)
+
+        @pl.when(m < NCH // 2)
+        def _():
+            late_out(m)
+            job_self.tile(2 * m)
+            job_self.tile(2 * m + 1)
+
+        @pl.when(m == 1)
+        def _():
+            job_out_b.s3()
+
+        @pl.when(m == 2)
+        def _():
+            job_in_b.s3()
+
+        @pl.when(m == NCH // 2)
+        def _():
+            job_self.start()
+            job_out_b.s4()
+
+        @pl.when(m == NCH // 2 + 1)
+        def _():
+            job_in_b.s4()
+
+        @pl.when(m == NCH // 2 + 2)
+        def _():
+            job_self.s1()
+            job_out_b.s5()
+
+        @pl.when(m == NCH // 2 + 3)
+        def _():
+            job_in_b.s5()
+
+    loop(0, NCH, sixth_chunk)
+    late_rows = [pl.ds(0, T // 2), pl.ds(T // 2, T // 2)]
+    late_cps = [
+        pltpu.make_async_copy(r.part.at[2, rw], r.latents_out.at[rw], r.out_sem.at[2 + k])
+        for k, rw in enumerate(late_rows)
+    ]
+    late_cps[0].start()
+
+    def seventh_chunk(m):
+        @pl.when(m < NCH - 2)
+        def _():
+            ar_b(1, m + 2)
+
+        @pl.when(is_mid & (m < NCH // 2))
+        def _():
+            cp_tot(2, m).wait_send()
+
+        ar_c(1, m, 0)
+        rw = rows(m)
+        dx = r.dxs[rw] + norm_grad(total_of(1, m), r.h1, 2, r.rs2, rw)
+        r.dxs[rw] = dx
+        low = dx.astype(bf16)
+        r.ra[rw] = low
+        r.do[1, rw] = dot_nn(low, r.woc[...]).astype(bf16)
+        d_o_cp(1, m).start()
+
+        @pl.when(m < NCH // 2)
+        def _():
+            job_out_a.tile(2 * m)
+            job_out_a.tile(2 * m + 1)
+
+        @pl.when(m == 0)
+        def _():
+            job_out_b.s6()
+            job_self.s2()
+
+        @pl.when(m == 1)
+        def _():
+            job_in_b.s6()
+
+        @pl.when(m == 2)
+        def _():
+            job_self.s3()
+
+        @pl.when(m == NCH // 2)
+        def _():
+            job_out_a.start()
+            job_self.s4()
+
+        @pl.when(m >= NCH // 2)
+        def _():
+            job_in_a.tile(2 * m - NCH)
+            job_in_a.tile(2 * m + 1 - NCH)
+
+        @pl.when(m == NCH // 2 + 2)
+        def _():
+            job_out_a.s1()
+            job_self.s5()
+
+    loop(0, NCH, seventh_chunk)
+    job_in_a.start()
+    late_sends(NCH // 2, NCH)
+
+    for hd in range(HL):
+        waits = [] if hd else [functools.partial(wait_d_o, 1)] + [cp.wait for cp in back_cross]
+        attend_back(
+            hd, r.do.at[1], r.do_o.at[1], r.q, r.qr_c, r.kv, r.p_c, r.pr_c, r.o_c, r.or_c, I, 0, r.dq, 0, r.dkv, 0,
+            (lambda: None) if hd else job_in_a.s1, waits,
+        )
+        if hd == 0:
+            ar_b(2, NCH // 2)
+            ar_b(2, NCH // 2 + 1)
+            job_out_a.s2()
+
+    late_cps[0].wait()
+    loop(0, ICH, lambda k: ar_put(2, k, dot_nt(r.dkv[rows(k)], r.wkvc[...])))
+    loop(0, NCH, lambda k: ar_put(0, k, dot_nt(r.dq[rows(k)], r.wqc[...])))
+    job_self.s6()
+    loop(0, D // LANES, job_cross.tile)
+    job_cross.start()
+    loop(NCH // 2 + 2, NCH, lambda c: ar_b(2, c))
+    loop(0, 2, lambda c: ar_b(2, c))
+    job_in_a.s2()
+    job_out_a.s3()
+
+    def input_chunk(m):
+        @pl.when(m < ICH - 2)
+        def _():
+            ar_b(2, m + 2)
+
+        @pl.when(m >= ICH - 2)
+        def _():
+            ar_b(0, m + 2 - ICH)
+
+        ar_c(2, m)
+        rw = rows(m)
+        r.gin[rw] = norm_grad(total_of(2, m), r.bn, 1, r.rs1, rw)
+
+    loop(0, ICH, input_chunk)
+    job_cross.s1()
+    job_in_a.s3()
+    job_out_a.s4()
+
+    def last_chunk(m):
+        @pl.when(m < NCH - 2)
+        def _():
+            ar_b(0, m + 2)
+
+        ar_c(0, m, 1)
+        rw = rows(m)
+        r.dxs[rw] += norm_grad(total_of(0, m), r.an, 0, r.rs0, rw)
+
+        @pl.when(m < NCH // 2)
+        def _():
+            late_out(m + NCH // 2)
+
+        @pl.when(m == 2)
+        def _():
+            job_cross.s2()
+            job_in_a.s4()
+
+        @pl.when(m == 3)
+        def _():
+            job_out_a.s5()
+
+        @pl.when(m == 5)
+        def _():
+            job_cross.s3()
+            job_in_a.s5()
+
+    loop(0, NCH, last_chunk)
+
+    outs = [
+        pltpu.make_async_copy(r.dxs, r.latent_grad, r.out_sem.at[0]),
+        pltpu.make_async_copy(r.gin, r.input_grad, r.out_sem.at[1]),
+        late_cps[1],
+    ]
+    for cp in outs:
+        cp.start()
+    for k, where in enumerate((at_core, at_x, at_y)):
+        cp = remote(r.dg, r.dgr.at[k], r.dg_snd.at[k], r.dg_rcv.at[k], where)
+        cp.start()
+        cp.wait()
+        r.dg[...] += r.dgr[k]
+        if k == 0:
+            job_cross.s4()
+            job_out_a.s6()
+    r.gains_grad[...] = r.dg[...]
+    job_cross.s5()
+    job_in_a.s6()
+    job_cross.s6()
+
+    @pl.when(is_mid)
+    def _():
+        loop(0, NCH, lambda c: cp_tot(2, c).wait_send())
+        loop(0, NCH, lambda c: cp_tot(0, c).wait_send())
+
+    for cp in outs:
+        cp.wait()
+
+
+def block_call(latents, inputs, latent_group, latent_valid, input_group, input_valid, gains, weights, out_grad):
+    T, D = latents.shape
+    I = inputs.shape[0]
+    C = weights["w_q_c"].shape[1]
+    F = weights["w_in_a"].shape[1]
+    CH = 64
+    NCH = T // CH
+    HL = C // HEAD_DIM
+    in_vmem = dict(
+        latent_group=latent_group, latent_valid=latent_valid, input_group=input_group,
+        input_valid=input_valid, gains=gains,
+    )
+    in_any = dict(latents=latents, inputs=inputs, **weights, out_grad=out_grad)
+    S = jax.ShapeDtypeStruct
+    out_any = dict(
+        latents_out=S((T, D), bf16), latent_grad=S((T, D), f32), input_grad=S((I, D), f32),
+        g_out_b=S((D, F), bf16), g_in_b=S((D, F), bf16), g_self=S((D, 4 * C), bf16),
+        g_out_a=S((D, F), bf16), g_in_a=S((D, F), bf16), g_cross=S((D, 4 * C), bf16),
+    )
+    out_vmem = dict(gains_grad=S((8, D), f32))
+    V, DMA = pltpu.VMEM, pltpu.SemaphoreType.DMA
+    half, eighth, piece = D // 2, D // 8, D // 16
+    scratch = dict(
+        inp=V((I, D), bf16), lat=V((T, D), bf16), r4=V((T, D), bf16),
+        wkvc=V((D, 2 * C), bf16), wqc=V((D, C), bf16), woc=V((D, C), bf16),
+        wina=V((D, F), bf16), wouta=V((D, F), bf16), wqkvs=V((D, 3 * C), bf16),
+        wos=V((D, C), bf16), winb=V((D, F), bf16), woutb=V((D, F), bf16), wj=V((D, F), bf16),
+        codes=V((8, I + 2 * T), f32), codes_o=V((8, I + 2 * T), f32),
+        qcol=V((T, LANES), f32), qcol_o=V((T, LANES), f32),
+        part=V((3, T, D), bf16), rin=V((3, T, D), bf16), rmid=V((3, T, D), bf16),
+        xs=V((T, D), f32), dxs=V((T, D), f32), gin=V((I, D), f32),
+        an=V((T, D), bf16), bn=V((I, D), bf16), h1=V((T, D), bf16), cs=V((T, D), bf16), h2=V((T, D), bf16),
+        rs0=V((T, LANES), f32), rs1=V((I, LANES), f32), rs2=V((T, LANES), f32), rs3=V((T, LANES), f32),
+        rs4=V((T, LANES), f32),
+        z1=V((T, F), bf16), s1=V((T, F), bf16), du1=V((T, F), bf16), z2=V((T, F), bf16), du2=V((T, F), bf16),
+        ra=V((T, D), bf16), rb=V((T, D), bf16),
+        q=V((T, C), bf16), kv=V((2 * I, 2 * C), bf16), p_c=V((HL, T, 2 * I), bf16), o_c=V((T, C), bf16),
+        q2=V((T, C), bf16), kv2=V((2 * T, 2 * C), bf16), p_s=V((HL, T, 2 * T), bf16), o_s=V((T, C), bf16),
+        pr_c=V((HL, T, I), bf16), qr_c=V((T, C), bf16), or_c=V((T, C), bf16),
+        pr_s=V((HL, T, T), bf16), qr_s=V((T, C), bf16), or_s=V((T, C), bf16),
+        do=V((2, T, C), bf16), do_o=V((2, T, C), bf16), ds=V((2 * T, max(T, I)), bf16),
+        dqkv=V((T, 3 * C), bf16), dq=V((T, C), bf16), dkv=V((I, 2 * C), bf16),
+        rc=V((3, half, F), bf16), r1p=V((3, eighth, F), bf16), r1q=V((3, eighth, F), bf16),
+        r2p=V((3, piece, F), bf16), r2q=V((3, piece, F), bf16),
+        dg=V((8, D), f32), dgr=V((3, 8, D), f32),
+        load_sem=DMA((16,)), out_sem=DMA((4,)),
+        y_snd=DMA((8,)), y_rcv=DMA((8,)),
+        kv_snd=DMA((NCH,)), kv_rcv=DMA((NCH,)), do_snd=DMA((2, NCH)), do_rcv=DMA((2, NCH)),
+        ar_snd=DMA((3, NCH)), ar_tot=DMA((3, NCH)), ar_in=DMA((3, NCH)), ar_mid=DMA((3, NCH)),
+        j_snd=DMA((6, 10)), j_rcv=DMA((6, 10)), j_own=DMA((6, 2)), dg_snd=DMA((3,)), dg_rcv=DMA((3,)),
+    )
+    names = [*in_vmem, *in_any, *out_any, *out_vmem, *scratch]
+    outs = pl.pallas_call(
+        functools.partial(block_kernel, names, T, I, D, C, F, CH),
+        out_shape=(*out_any.values(), *out_vmem.values()),
+        in_specs=[pl.BlockSpec(memory_space=pltpu.VMEM)] * len(in_vmem)
+        + [pl.BlockSpec(memory_space=pl.ANY)] * len(in_any),
+        out_specs=tuple(
+            [pl.BlockSpec(memory_space=pl.ANY)] * len(out_any)
+            + [pl.BlockSpec(memory_space=pltpu.VMEM)] * len(out_vmem)
+        ),
+        scratch_shapes=list(scratch.values()),
+        compiler_params=pltpu.CompilerParams(
+            collective_id=0, has_side_effects=True, vmem_limit_bytes=63 * 2**20
+        ),
+        name="block_kernel",
+    )(*in_vmem.values(), *in_any.values())
+    return dict(zip([*out_any, *out_vmem], outs, strict=True))
+
+
+def per_device_fast(
+    latents, inputs, latent_group, latent_valid, input_group, input_valid, gains,
+    w_q_cross, w_kv_cross, w_o_cross, w_in_a, w_out_a, w_qkv_self, w_o_self, w_in_b, w_out_b, out_grad,
+):
+    D = latents.shape[2]
+    C = w_q_cross.shape[1]
+    weights = dict(
+        w_q_c=w_q_cross, w_kv_c=w_kv_cross.reshape(D, 2 * C), w_o_c=w_o_cross, w_in_a=w_in_a,
+        w_out_a=w_out_a, w_qkv_s=w_qkv_self.reshape(D, 3 * C), w_o_s=w_o_self, w_in_b=w_in_b, w_out_b=w_out_b,
+    )
+    o = block_call(
+        latents[0], inputs[0], latent_group, latent_valid, input_group, input_valid, gains, weights, out_grad[0]
+    )
+    g_cross, g_self = o["g_cross"], o["g_self"]
+    return (
+        o["latents_out"][None],
+        o["latent_grad"][None],
+        o["input_grad"][None],
+        o["gains_grad"][: gains.shape[0]],
+        g_cross[:, 2 * C : 3 * C].astype(f32),
+        g_cross[:, : 2 * C].astype(f32).reshape(D, 2, C),
+        g_cross[:, 3 * C :].astype(f32),
+        o["g_in_a"].astype(f32),
+        o["g_out_a"].astype(f32),
+        g_self[:, : 3 * C].astype(f32).reshape(D, 3, C),
+        g_self[:, 3 * C :].astype(f32),
+        o["g_in_b"].astype(f32),
+        o["g_out_b"].astype(f32),
+    )
+
+
 def solution(mesh):
+    fast = dict(mesh.shape) == {"group": 4, "blk": 2, "head": 4}
     return jax.shard_map(
-        per_device,
+        per_device_fast if fast else per_device,
         mesh=mesh,
         in_specs=(
             P("group", "blk", None),

time: 1660 us -> 344 us (0.21)
  waiting for transfers between devices: 1310 us -> 0 us
  Pallas kernels: 0 us -> 309 us
  blocking collectives: 108 us -> 0 us
  matrix products: 107 us -> 0 us
  local copies, waits for them, and re-layouts: 68.7 us -> 18.9 us
  other arithmetic: 46.2 us -> 14.9 us
    psum x7 -> x0, waiting for transfers between devices: 673 us -> none  [the longest x4 444 us: head_sum(): return lax.psum(partial_sum, 'head')]
    reduce_scatter x10 -> x0, waiting for transfers between devices: 359 us -> none  [the longest x1 55.5 us: per_device(): lax.psum_scatter(grad_out_a, ('group', 'blk'), scatter_dimension=0, tiled...]
    pallas_call x0 -> x1, Pallas kernels: none -> 309 us  [block_call(): pl.pallas_call(functools.partial(block_kernel, names, T, I, D, C, F, CH),...]
    all_gather x9 -> x0, waiting for transfers between devices: 273 us -> none  [the longest x1 39.4 us: per_device(): lax.all_gather(sum_out_b, ('group', 'blk'), axis=0, tiled=True)]
    all_gather x16 -> x0, blocking collectives: 108 us -> none  [the longest x2 18.1 us: attend_back(): lax.all_gather(queries, 'blk', axis=0, tiled=True)]
    dot_general x39 -> x0, matrix products: 107 us -> none  [the longest x9 25.3 us: out_product(): lax.dot_general(left, right, contract_last, preferred_element_type=jnp.fl...]
    unnamed x272 -> x27, local copies, waits for them, and re-layouts: 56.4 us -> 12.6 us
    reduce_sum x22 -> x0, other arithmetic: 29 us -> none  [the longest x7 15.6 us: layer_norm(): return centred * lax.rsqrt(variance + 1e-05) * gains_row]
  transfers between devices with their start and end apart: 26 -> 0, of which waited for: 24 -> 0; matrix products, arithmetic and copies ran while one was open for 6% -> 0% of each run, Pallas kernels for 0% -> 0%
where the time goes in v1:
time: 344 us
  Pallas kernels  309 us (90%)
  local copies, waits for them, and re-layouts  18.9 us (5%)
  other arithmetic  14.9 us (4%)
    pallas_call x1, Pallas kernels, block_call(): pl.pallas_call(functools.partial(block_kernel, names, T, I, D, C, F, CH),...  309 us
    unnamed x27, local copies, waits for them, and re-layouts  12.6 us

profile of v1, /device:TPU:0, one launch (start us, length us, event | category | flops | bytes accessed | tf_op | source)
XLA Modules:
  0.0 343.7 jit_solution(4539176234989409704)
XLA Ops:
  0.6 0.0 copy-start.6
  0.7 2.5 copy.36
  3.2 0.0 copy-done.6
  3.2 0.9 copy.32
  4.1 1.6 copy.33.refs_12_
  5.6 309.2 %block_kernel.1 = (bf16[512,1024]{1,0:T(8,128)(2,1)}, f32[512,1024]{1,0:T(8,128)}, f32[256,1024]{1,0:T(8,128)}, bf16[1024,1024]{1,0:T(8,128)(2,1)}, bf16[1024,10...) custom-call(s32[1,512]{1,0:T(1,128)} %refs_0_.1, ...), custom_call_target="tpu_custom_call" | custom-call | tf_op jit(solution)/shard_map/block_kernel/pallas_call | solution.py:1339
  314.8 1.5 slice_convert_fusion.1
  316.3 2.4 reshape.51
  318.7 3.3 slice_convert_fusion.3
  322.0 0.0 copy-done.5
  322.0 0.2 slice_convert_fusion
  322.2 2.4 copy.34
  324.6 0.0 copy-start.3
  324.6 3.7 %copy.35 = f32[1024,3,256]{2,0,1:T(8,128)} copy(f32[1024,3,256]{0,2,1:T(8,128)} %bitcast.11) | data formatting | bytes 6291456
  328.3 0.0 copy-done.3
  328.3 0.0 copy-start.2
  328.3 2.5 convert_element_type.25
  330.8 0.0 copy-done.2
  330.8 0.0 copy-start.1
  330.8 2.5 convert_element_type.26
  333.2 0.0 copy-done.1
  333.2 2.5 convert_element_type.28
  335.7 0.0 copy-done
  335.7 2.5 convert_element_type.29
  338.2 0.0 copy-done.8
  338.2 1.0 copy.41
  339.2 1.0 copy-done.4
  340.2 1.3 copy.42
  341.5 0.6 copy-done.7
  342.1 1.0 copy.43
  343.1 0.0 copy-done.9
  343.1 0.6 copy.44
  (6 shorter events, 0.0 us)
Async XLA Ops:
  0.6 2.6 copy-start.6
  318.7 3.3 copy-start.5
  324.6 3.7 %copy-start.3 = (bf16[1024,1024]{1,0:T(8,128)(2,1)S(1)}, bf16[1024,1024]{1,0:T(8,128)(2,1)}, u32[]{:S(2)}) copy-start(bf16[1024,1024]{1,0:T(8,128)(2,1)} %get-tuple-element.28) | copy-start | bytes 6291460
  328.3 2.5 copy-start.2
  330.8 2.5 copy-start.1
  333.2 2.5 copy-start
  335.7 2.5 copy-start.8
  338.2 2.0 copy-start.4
  340.2 2.0 copy-start.7
  342.1 1.0 copy-start.9

commit v2 on v1

--- a/solution.py
+++ b/solution.py
@@ -510,6 +510,7 @@
 MESH = pl.DeviceIdType.MESH
 bf16, f32 = jnp.bfloat16, jnp.float32
 LANES = 128
+TILE = 256
 SCALE = HEAD_DIM**-0.5
 GELU_A = 0.7978845608028654
 GELU_B = 0.044715
@@ -547,6 +548,22 @@
         return carry
 
     lax.fori_loop(start, stop, step, 0)
+
+
+SCHEDULE = dict(
+    fifth=["At", "Bt", "A1", "", "B1", "", "", ""],
+    self_keys_0=[""],
+    self_keys_1=["A2"],
+    sixth_put=["B2 St"],
+    sixth=["A3", "B3 S1", "A4", "B4", "S2", "A5", "S3", "B5"],
+    seventh=["Ct S4", "Dt", "C1 A6", "", "D1", "B6", "", ""],
+    cross_keys_0=["C2"],
+    cross_keys_1=["D2 S5"],
+    last_put=["Xt C3 D3"],
+    input=["X1 C4", "gz1 D4", "S6 C5", "gz2 X2"],
+    last=["D5", "X3 gz3 dg0", "C6", "X4 dg1", "D6", "dg2", "X5", "dg3"],
+    end=["X6"],
+)
 
 
 def block_kernel(names, T, I, D, C, F, CH, *refs):
@@ -598,7 +615,8 @@
     load(r.w_o_c, r.woc, "woc")
     load(r.w_in_a, r.wina, "wina")
     load(r.w_out_a, r.wouta, "wouta")
-    load(r.w_qkv_s, r.wqkvs, "wqkvs")
+    for j in range(3):
+        load(r.w_qkv_s.at[j], r.wqkvs.at[:, pl.ds(j * C, C)], "wqkvs%d" % j)
     load(r.w_o_s, r.wos, "wos")
     load(r.w_in_b, r.winb, "winb")
     load(r.w_out_b, r.woutb, "woutb")
@@ -620,6 +638,7 @@
 
     make_columns(lgf, r.qcol)
     r.dg[...] = jnp.zeros_like(r.dg)
+    r.gz[...] = jnp.zeros_like(r.gz)
 
     @pl.when(is_mid)
     def _():
@@ -635,19 +654,29 @@
     codes_cp = to_y(r.codes, r.codes_o, 0)
     codes_cp.start()
 
+    SUB = 2
+    SR = CH // SUB
+
     def cp_in(p, c):
-        return remote(r.part.at[p, rows(c)], r.rin.at[p, rows(c)], r.ar_snd.at[p, c], r.ar_in.at[p, c], at_pair)
+        rw = rows(c, SR)
+        return remote(r.part.at[p, rw], r.rin.at[p, rw], r.ar_snd.at[p, c], r.ar_in.at[p, c], at_pair)
 
     def cp_mid(p, c):
-        return remote(r.part.at[p, rows(c)], r.rmid.at[p, rows(c)], r.ar_snd.at[p, c], r.ar_mid.at[p, c], at_mid)
+        rw = rows(c, SR)
+        return remote(r.part.at[p, rw], r.rmid.at[p, rw], r.ar_snd.at[p, c], r.ar_mid.at[p, c], at_mid)
 
     def cp_tot(p, c):
-        return remote(r.rin.at[p, rows(c)], r.rin.at[p, rows(c)], r.ar_tot.at[p, c], r.ar_in.at[p, c], at_pair)
+        rw = rows(c, SR)
+        return remote(r.rin.at[p, rw], r.rin.at[p, rw], r.ar_tot.at[p, c], r.ar_in.at[p, c], at_pair)
+
+    def subs(c):
+        return [c * SUB + k for k in range(SUB)]
 
     def ar_send(p, c):
         @pl.when(is_end)
         def _():
-            cp_in(p, c).start()
+            for k in subs(c):
+                cp_in(p, k).start()
 
     def ar_put(p, c, value):
         r.part[p, rows(c)] = value.astype(bf16)
@@ -656,26 +685,35 @@
     def ar_b(p, c):
         @pl.when(is_mid)
         def _():
-            cp_in(p, c).wait_recv()
-            total = r.part[p, rows(c)].astype(f32) + r.rin[p, rows(c)].astype(f32)
-            r.part[p, rows(c)] = total.astype(bf16)
-            cp_mid(p, c).start()
+            for k in subs(c):
+                rw = rows(k, SR)
+                cp_in(p, k).wait_recv()
+                r.part[p, rw] = r.part[p, rw] + r.rin[p, rw]
+                cp_mid(p, k).start()
 
     def ar_c(p, c, prev=None):
         @pl.when(is_mid)
         def _():
-            cp_mid(p, c).wait_recv()
-            cp_mid(p, c).wait_send()
-            total = r.part[p, rows(c)].astype(f32) + r.rmid[p, rows(c)].astype(f32)
-            r.rin[p, rows(c)] = total.astype(bf16)
-            if prev is not None:
-                cp_tot(prev, c).wait_send()
-            cp_tot(p, c).start()
+            for k in subs(c):
+                rw = rows(k, SR)
+                cp_mid(p, k).wait_recv()
+                cp_mid(p, k).wait_send()
+                r.rin[p, rw] = r.part[p, rw] + r.rmid[p, rw]
+                if prev is not None:
+                    cp_tot(prev, k).wait_send()
+                cp_tot(p, k).start()
 
         @pl.when(is_end)
         def _():
-            cp_in(p, c).wait_send()
-            cp_tot(p, c).wait_recv()
+            for k in subs(c):
+                cp_in(p, k).wait_send()
+                cp_tot(p, k).wait_recv()
+
+    def drain(p, c):
+        @pl.when(is_mid)
+        def _():
+            for k in subs(c):
+                cp_tot(p, k).wait_send()
 
     def total_of(p, c):
         return r.rin[p, rows(c)].astype(f32)
@@ -694,12 +732,17 @@
         return pl.ds(pl.multiple_of(start, piece), n)
 
     class Job:
-        def __init__(self, index, w, slot, out, parts):
-            self.j, self.w, self.s, self.out, self.parts = index, w, slot, out, parts
+        def __init__(self, index, w, rc, out, parts):
+            self.j, self.w, self.rc, self.out, self.parts = index, w, rc, out, parts
+            self.s = index % 3
+
+        def tiles(self):
+            loop(0, D // TILE, self.tile)
+            self.cp_core().start()
 
         def tile(self, t):
             col = 0
-            rw = rows(t, LANES)
+            rw = rows(t, TILE)
             for lhs, rhs in self.parts:
                 n = rhs.shape[1]
                 self.w[rw, col : col + n] = dot_tn(lhs[:, rw], rhs[...]).astype(bf16)
@@ -709,7 +752,7 @@
             return remote(src, dst, r.j_snd.at[self.j, k], r.j_rcv.at[self.j, k], where)
 
         def cp_core(self):
-            return self.cp(0, self.w.at[span((1 - core) * half, half)], r.rc.at[self.s], at_core)
+            return self.cp(0, self.w.at[span((1 - core) * half, half)], self.rc, at_core)
 
         def cp_p1(self):
             return self.cp(1, self.w.at[span(p_oth, eighth)], r.r1p.at[self.s], at_x)
@@ -750,26 +793,23 @@
 
         def add(self, start, n, other):
             rw = span(start, n)
-            self.w[rw] = (self.w[rw].astype(f32) + other[...].astype(f32)).astype(bf16)
-
-        def start(self):
-            self.cp_core().start()
+            self.w[rw] = self.w[rw] + other[...]
 
         def s1(self):
             self.cp_core().wait_recv()
-            self.add(p_oth, eighth, r.rc.at[self.s, span(p_oth - own, eighth)])
+            self.add(p_oth, eighth, self.rc.at[span(p_oth - own, eighth)])
             self.cp_p1().start()
-            self.add(q_oth, eighth, r.rc.at[self.s, span(q_oth - own, eighth)])
+            self.add(q_oth, eighth, self.rc.at[span(q_oth - own, eighth)])
             self.cp_q1().start()
-            self.add(p_own, eighth, r.rc.at[self.s, span(p_own - own, eighth)])
-            self.add(q_own, eighth, r.rc.at[self.s, span(q_own - own, eighth)])
+            self.add(p_own, eighth, self.rc.at[span(p_own - own, eighth)])
+            self.add(q_own, eighth, self.rc.at[span(q_own - own, eighth)])
 
         def s2(self):
             self.cp_p1().wait_recv()
             self.add(p_own, eighth, r.r1p.at[self.s])
-            self.cp_p2().start()
             self.cp_q1().wait_recv()
             self.add(q_own, eighth, r.r1q.at[self.s])
+            self.cp_p2().start()
             self.cp_q2().start()
 
         def s3(self):
@@ -802,12 +842,12 @@
         def s6(self):
             self.cp_all().wait()
 
-    job_out_b = Job(0, r.woutb, 0, r.g_out_b, [(r.r4, r.z2)])
-    job_in_b = Job(1, r.winb, 1, r.g_in_b, [(r.h2, r.du2)])
-    job_self = Job(2, r.wj, 2, r.g_self, [(r.cs, r.dqkv), (r.ra, r.o_s)])
-    job_out_a = Job(3, r.woutb, 0, r.g_out_a, [(r.rb, r.z1)])
-    job_in_a = Job(4, r.winb, 1, r.g_in_a, [(r.h1, r.du1)])
-    job_cross = Job(5, r.wj, 2, r.g_cross, [(r.bn, r.dkv), (r.an, r.dq), (r.ra, r.o_c)])
+    job_out_b = Job(0, r.woutb, r.rc.at[0], r.g_out_b, [(r.r4, r.z2)])
+    job_in_b = Job(1, r.winb, r.rc.at[1], r.g_in_b, [(r.h2, r.du2)])
+    job_self = Job(2, r.wj, r.rc.at[2], r.g_self, [(r.cs, r.dqkv), (r.ra, r.o_s)])
+    job_out_a = Job(3, r.p_s, r.z2, r.g_out_a, [(r.rb, r.z1)])
+    job_in_a = Job(4, r.woutb, r.du2, r.g_in_a, [(r.h1, r.du1)])
+    job_cross = Job(5, r.winb, r.h2, r.g_cross, [(r.bn, r.dkv), (r.an, r.dq), (r.ra, r.o_c)])
 
     def norm_out(x, gain_row, out, rstd_out, rw):
         xhat, rstd = norm_rows(x)
@@ -816,13 +856,14 @@
         out[rw] = low
         return low
 
-    def norm_grad(cot, low_ref, gain_row, rstd_ref, rw):
+    def norm_grad(cot, low_ref, dg_row, gain_row, rstd_ref, rw):
         gain = gains[gain_row : gain_row + 1, :]
         xhat = low_ref[rw].astype(f32) * (1.0 / gain)
         scaled = cot * gain
         mean_one = jnp.mean(scaled, axis=-1, keepdims=True)
         mean_two = jnp.mean(scaled * xhat, axis=-1, keepdims=True)
-        r.dg[gain_row : gain_row + 1, :] += jnp.sum(cot * xhat, axis=0, keepdims=True)
+        if dg_row is not None:
+            r.dg[dg_row : dg_row + 1, :] += jnp.sum(cot * xhat, axis=0, keepdims=True)
         return rstd_ref[rw, 0:1] * (scaled - mean_one - xhat * mean_two)
 
     loads["inp"].wait()
@@ -860,7 +901,7 @@
             s = jnp.where(allowed, dot_nt(q_ref[rw, cols], kv_ref[:, cols]) * SCALE, masked_fill)
             e = jnp.exp(s - jnp.max(s, axis=-1, keepdims=True))
             p = (e * (1.0 / jnp.sum(e, axis=-1, keepdims=True))).astype(bf16)
-            p_ref[hd, rw, :] = p
+            p_ref[rows(k + hd * NCH), :] = p
             o_ref[rw, cols] = dot_nn(p, kv_ref[:, vcols]).astype(bf16)
 
     def cross_chunk(k):
@@ -872,8 +913,9 @@
             ar_b(0, k - 4)
 
     loop(0, NCH, cross_chunk)
+
     back_cross = [
-        to_y(r.p_c.at[:, :, pl.ds(I, I)], r.pr_c, 2), to_y(r.q, r.qr_c, 3), to_y(r.o_c, r.or_c, 4),
+        to_y(r.p_c.at[:, pl.ds(I, I)], r.pr_c, 2), to_y(r.q, r.qr_c, 3), to_y(r.o_c, r.or_c, 4),
     ]
     for cp in back_cross:
         cp.start()
@@ -901,7 +943,8 @@
             ar_b(1, m + 2 - NCH)
 
     loop(0, NCH, first_chunk)
-    loads["wqkvs"].wait()
+    for j in range(3):
+        loads["wqkvs%d" % j].wait()
     loads["wos"].wait()
 
     def kv2_cp(c):
@@ -925,8 +968,17 @@
     loop(0, NCH, second_chunk)
     loop(0, NCH, lambda c: kv2_cp(c).wait())
 
+    def p_cp(c):
+        return remote(r.p_s.at[rows(c), pl.ds(T, T)], r.pr_s.at[rows(c)], r.p_snd.at[c], r.p_rcv.at[c], at_y)
+
+    q_back = to_y(r.q2, r.qr_s, 6)
+    q_back.start()
+
     def self_chunk(k):
         attend_chunk(k, r.q2, r.kv2, r.p_s, r.o_s, I, T)
+        for hd in range(HL):
+            p_cp(k + hd * NCH).start()
+
         ar_put(0, k, dot_nt(r.o_s[rows(k)], r.wos[...]))
 
         @pl.when(k >= 4)
@@ -934,11 +986,8 @@
             ar_b(0, k - 4)
 
     loop(0, NCH, self_chunk)
-    back_self = [
-        to_y(r.p_s.at[:, :, pl.ds(T, T)], r.pr_s, 5), to_y(r.q2, r.qr_s, 6), to_y(r.o_s, r.or_s, 7),
-    ]
-    for cp in back_self:
-        cp.start()
+    o_back = to_y(r.o_s, r.or_s, 7)
+    o_back.start()
     loads["winb"].wait()
     loads["woutb"].wait()
     loads["r4"].wait()
@@ -970,6 +1019,102 @@
     def d_o_cp(k, c):
         return remote(r.do.at[k, rows(c)], r.do_o.at[k, rows(c)], r.do_snd.at[k, c], r.do_rcv.at[k, c], at_y)
 
+    class Back:
+        def __init__(self, k, q, qr, kv, p, pr, o, o_r, n, start, dq, dkv, dkv_col):
+            self.k, self.q, self.qr, self.kv, self.p, self.pr, self.o, self.o_r = k, q, qr, kv, p, pr, o, o_r
+            self.n, self.first, self.dq, self.dkv, self.dkv_col = n, start, dq, dkv, dkv_col
+            self.do, self.do_o = r.do.at[k], r.do_o.at[k]
+
+        def own(self, m):
+            rw = rows(m)
+            n, a = self.n, self.first
+            kc = jnp.concatenate([r.codes[0:1, a : a + n], r.codes_o[0:1, a : a + n]], axis=1)
+            allowed = r.qcol[rw, 0:1] == kc
+            for hd in range(HL):
+                cols = slice(hd * HEAD_DIM, (hd + 1) * HEAD_DIM)
+                vcols = slice(C + hd * HEAD_DIM, C + (hd + 1) * HEAD_DIM)
+                grad = self.do[rw, cols]
+                delta = jnp.sum(grad.astype(f32) * self.o[rw, cols].astype(f32), axis=-1, keepdims=True)
+                diff = dot_nt(grad, self.kv[:, vcols]) - delta
+                prob = self.p[rows(m + hd * NCH), :].astype(f32)
+                ds = jnp.where(allowed, prob * diff, 0.0).astype(bf16)
+                r.ds[rows(m + 2 * hd * NCH), 0:n] = ds[:, 0:n]
+                self.dq[rw, cols] = (dot_nn(ds, self.kv[:, cols]) * SCALE).astype(bf16)
+
+        def other(self, m):
+            d_o_cp(self.k, m).wait()
+            rw = rows(m)
+            n, a = self.n, self.first
+            allowed = r.qcol_o[rw, 0:1] == r.codes[0:1, a : a + n]
+            for hd in range(HL):
+                cols = slice(hd * HEAD_DIM, (hd + 1) * HEAD_DIM)
+                vcols = slice(C + hd * HEAD_DIM, C + (hd + 1) * HEAD_DIM)
+                grad = self.do_o[rw, cols]
+                delta = jnp.sum(grad.astype(f32) * self.o_r[rw, cols].astype(f32), axis=-1, keepdims=True)
+                diff = dot_nt(grad, self.kv[0:n, vcols]) - delta
+                prob = self.pr[rows(m + hd * NCH), :].astype(f32)
+                ds = jnp.where(allowed, prob * diff, 0.0).astype(bf16)
+                r.ds[rows(m + (2 * hd + 1) * NCH), 0:n] = ds
+
+        def some_other(self, m, waits):
+            if waits is not None:
+
+                @pl.when(m == NCH // 2)
+                def _():
+                    for wait in waits:
+                        wait()
+
+            @pl.when((m >= NCH // 2) & (m < NCH - 2))
+            def _():
+                self.other(2 * m - NCH)
+                self.other(2 * m + 1 - NCH)
+
+            @pl.when(m == NCH - 2)
+            def _():
+                self.other(NCH - 4)
+
+            @pl.when(m == NCH - 1)
+            def _():
+                self.other(NCH - 3)
+
+        def keys(self, hd):
+            if hd >= HL:
+                return
+            n = self.n
+            cols = slice(hd * HEAD_DIM, (hd + 1) * HEAD_DIM)
+            at = 2 * hd * T
+            dk = dot_tn(r.ds[at : at + T, 0:n], self.q[:, cols]) + dot_tn(r.ds[at + T : at + 2 * T, 0:n], self.qr[:, cols])
+            col = self.dkv_col + hd * HEAD_DIM
+            self.dkv[:, col : col + HEAD_DIM] = (dk * SCALE).astype(bf16)
+            at = hd * T
+            dv = dot_tn(self.p[at : at + T, 0:n], self.do[:, cols]) + dot_tn(self.pr[at : at + T, :], self.do_o[:, cols])
+            col += C
+            self.dkv[:, col : col + HEAD_DIM] = dv.astype(bf16)
+
+    back_of_self = Back(0, r.q2, r.qr_s, r.kv2, r.p_s, r.pr_s, r.o_s, r.or_s, T, I, r.dqkv, r.dqkv, C)
+    back_of_cross = Back(1, r.q, r.qr_c, r.kv, r.p_c, r.pr_c, r.o_c, r.or_c, I, 0, r.dq, r.dkv, 0)
+
+    jobs = dict(A=job_out_b, B=job_in_b, S=job_self, C=job_out_a, D=job_in_a, X=job_cross)
+    extra = {}
+
+    def on(place, m=None):
+        for step, words in enumerate(SCHEDULE[place]):
+            names = words.split()
+            if not names:
+                continue
+
+            def run(names=names):
+                for name in names:
+                    if name in extra:
+                        extra[name]()
+                    else:
+                        getattr(jobs[name[0]], "tiles" if name[1] == "t" else "s" + name[1])()
+
+            if m is None:
+                run()
+            else:
+                pl.when(m == step)(run)
+
     def fifth_chunk(m):
         @pl.when(m < NCH - 2)
         def _():
@@ -977,99 +1122,48 @@
 
         ar_c(1, m, 0)
         rw = rows(m)
-        dx = r.r4[rw].astype(f32) + norm_grad(total_of(1, m), r.h2, 4, r.rs4, rw)
+        dx = r.r4[rw].astype(f32) + norm_grad(total_of(1, m), r.h2, 4, 4, r.rs4, rw)
         r.dxs[rw] = dx
         low = dx.astype(bf16)
         r.ra[rw] = low
         r.do[0, rw] = dot_nn(low, r.wos[...]).astype(bf16)
         d_o_cp(0, m).start()
-
-        @pl.when(m < NCH // 2)
-        def _():
-            job_out_b.tile(2 * m)
-            job_out_b.tile(2 * m + 1)
-
-        @pl.when(m == NCH // 2)
-        def _():
-            job_out_b.start()
+        back_of_self.own(m)
+        back_of_self.some_other(m, [q_back.wait, o_back.wait, lambda: loop(0, HL * NCH, lambda c: p_cp(c).wait())])
+
+        on("fifth", m)
 
         @pl.when(m >= NCH // 2)
         def _():
-            job_in_b.tile(2 * m - NCH)
-            job_in_b.tile(2 * m + 1 - NCH)
-
+            ar_b(2, m - NCH // 2)
+
+    loop(0, NCH // 2, lambda c: ar_send(2, c))
     loop(0, NCH, fifth_chunk)
-    job_in_b.start()
-
-    def late_sends(lo, hi):
-        loop(lo, hi, lambda c: ar_send(2, c))
 
     def late_out(c):
         ar_c(2, c)
         rw = rows(c)
         r.part[2, rw] = (r.xs[rw] + total_of(2, c)).astype(bf16)
 
-    late_sends(0, NCH // 2)
-
-    QB = 128
-
-    def attend_back(hd, do, do_o, q_ref, qr_ref, kv_ref, p_ref, pr_ref, o_ref, or_ref, n, start, dq_ref, dq_col, dkv_ref, dkv_col, between, waits):
-        cols = slice(hd * HEAD_DIM, (hd + 1) * HEAD_DIM)
-        vcols = slice(C + hd * HEAD_DIM, C + (hd + 1) * HEAD_DIM)
-
-        def own_queries(k):
-            rw = rows(k, QB)
-            grad = do[rw, cols]
-            delta = jnp.sum(grad.astype(f32) * o_ref[rw, cols].astype(f32), axis=-1, keepdims=True)
-            kc = jnp.concatenate([r.codes[0:1, start : start + n], r.codes_o[0:1, start : start + n]], axis=1)
-            diff = dot_nt(grad, kv_ref[:, vcols]) - delta
-            ds = jnp.where(r.qcol[rw, 0:1] == kc, p_ref[hd, rw, :].astype(f32) * diff, 0.0).astype(bf16)
-            r.ds[rw, 0:n] = ds[:, 0:n]
-            dq_ref[rw, dq_col + hd * HEAD_DIM : dq_col + (hd + 1) * HEAD_DIM] = (
-                dot_nn(ds, kv_ref[:, cols]) * SCALE
-            ).astype(bf16)
-
-        loop(0, T // QB, own_queries)
-        between()
-        for wait in waits:
-            wait()
-
-        def other_queries(k):
-            rw = rows(k, QB)
-            grad = do_o[rw, cols]
-            delta = jnp.sum(grad.astype(f32) * or_ref[rw, cols].astype(f32), axis=-1, keepdims=True)
-            diff = dot_nt(grad, kv_ref[0:n, vcols]) - delta
-            allowed = r.qcol_o[rw, 0:1] == r.codes[0:1, start : start + n]
-            ds = jnp.where(allowed, pr_ref[hd, rw, :].astype(f32) * diff, 0.0).astype(bf16)
-            r.ds[rows(k + T // QB, QB), 0:n] = ds
-
-        loop(0, T // QB, other_queries)
-        dk = dot_tn(r.ds[0:T, 0:n], q_ref[:, cols]) + dot_tn(r.ds[T : 2 * T, 0:n], qr_ref[:, cols])
-        dkv_ref[:, dkv_col + hd * HEAD_DIM : dkv_col + (hd + 1) * HEAD_DIM] = (dk * SCALE).astype(bf16)
-        dv = dot_tn(p_ref[hd, :, 0:n], do[:, cols]) + dot_tn(pr_ref[hd], do_o[:, cols])
-        dkv_ref[:, dkv_col + C + hd * HEAD_DIM : dkv_col + C + (hd + 1) * HEAD_DIM] = dv.astype(bf16)
-
-    def wait_d_o(k):
-        loop(0, NCH, lambda c: d_o_cp(k, c).wait())
-
-    for hd in range(HL):
-        waits = [] if hd else [functools.partial(wait_d_o, 0)] + [cp.wait for cp in back_self]
-        attend_back(
-            hd, r.do.at[0], r.do_o.at[0], r.q2, r.qr_s, r.kv2, r.p_s, r.pr_s, r.o_s, r.or_s, T, I, r.dqkv, 0, r.dqkv, C,
-            (lambda: None) if hd else job_out_b.s1, waits,
-        )
-        if hd == 0:
-            ar_b(2, 0)
-            ar_b(2, 1)
-            job_in_b.s1()
+    back_of_self.other(NCH - 2)
+    back_of_self.other(NCH - 1)
+    back_of_self.keys(0)
+    on("self_keys_0")
+    loop(0, 2, late_out)
+    back_of_self.keys(1)
+    on("self_keys_1")
+    loop(2, NCH // 2, late_out)
+    late_cps = [
+        pltpu.make_async_copy(r.part.at[2, rw], r.latents_out.at[rw], r.out_sem.at[2 + 2 * k])
+        for k, rw in enumerate([pl.ds(0, T // 2), pl.ds(T // 2, T // 2)])
+    ]
+    late_cps[0].start()
 
     def sixth_put(k):
         ar_put(0, k, dot_nt(r.dqkv[rows(k)], r.wqkvs[...]))
 
     loop(0, NCH, sixth_put)
-    job_out_b.s2()
-    loop(2, NCH // 2, lambda c: ar_b(2, c))
-    job_in_b.s2()
+    on("sixth_put")
     loop(0, 2, lambda c: ar_b(0, c))
 
     def sixth_chunk(m):
@@ -1079,7 +1173,7 @@
 
         ar_c(0, m, 1)
         rw = rows(m)
-        dx = r.dxs[rw] + norm_grad(total_of(0, m), r.cs, 3, r.rs3, rw)
+        dx = r.dxs[rw] + norm_grad(total_of(0, m), r.cs, 3, 3, r.rs3, rw)
         r.dxs[rw] = dx
         low = dx.astype(bf16)
         r.rb[rw] = low
@@ -1091,122 +1185,109 @@
         def _():
             ar_b(1, m + 2 - NCH)
 
-        @pl.when(m < NCH // 2)
-        def _():
-            late_out(m)
-            job_self.tile(2 * m)
-            job_self.tile(2 * m + 1)
-
-        @pl.when(m == 1)
-        def _():
-            job_out_b.s3()
-
-        @pl.when(m == 2)
-        def _():
-            job_in_b.s3()
-
-        @pl.when(m == NCH // 2)
-        def _():
-            job_self.start()
-            job_out_b.s4()
-
-        @pl.when(m == NCH // 2 + 1)
-        def _():
-            job_in_b.s4()
-
-        @pl.when(m == NCH // 2 + 2)
-        def _():
-            job_self.s1()
-            job_out_b.s5()
-
-        @pl.when(m == NCH // 2 + 3)
-        def _():
-            job_in_b.s5()
+        on("sixth", m)
 
     loop(0, NCH, sixth_chunk)
-    late_rows = [pl.ds(0, T // 2), pl.ds(T // 2, T // 2)]
-    late_cps = [
-        pltpu.make_async_copy(r.part.at[2, rw], r.latents_out.at[rw], r.out_sem.at[2 + k])
-        for k, rw in enumerate(late_rows)
-    ]
-    late_cps[0].start()
-
     def seventh_chunk(m):
         @pl.when(m < NCH - 2)
         def _():
             ar_b(1, m + 2)
 
-        @pl.when(is_mid & (m < NCH // 2))
-        def _():
-            cp_tot(2, m).wait_send()
+        @pl.when(m < NCH // 2)
+        def _():
+            drain(2, m)
 
         ar_c(1, m, 0)
         rw = rows(m)
-        dx = r.dxs[rw] + norm_grad(total_of(1, m), r.h1, 2, r.rs2, rw)
+        dx = r.dxs[rw] + norm_grad(total_of(1, m), r.h1, 2, 2, r.rs2, rw)
         r.dxs[rw] = dx
         low = dx.astype(bf16)
         r.ra[rw] = low
         r.do[1, rw] = dot_nn(low, r.woc[...]).astype(bf16)
         d_o_cp(1, m).start()
-
-        @pl.when(m < NCH // 2)
-        def _():
-            job_out_a.tile(2 * m)
-            job_out_a.tile(2 * m + 1)
-
-        @pl.when(m == 0)
-        def _():
-            job_out_b.s6()
-            job_self.s2()
-
-        @pl.when(m == 1)
-        def _():
-            job_in_b.s6()
-
-        @pl.when(m == 2)
-        def _():
-            job_self.s3()
-
-        @pl.when(m == NCH // 2)
-        def _():
-            job_out_a.start()
-            job_self.s4()
+        back_of_cross.own(m)
+        back_of_cross.some_other(m, [cp.wait for cp in back_cross])
+
+        on("seventh", m)
 
         @pl.when(m >= NCH // 2)
         def _():
-            job_in_a.tile(2 * m - NCH)
-            job_in_a.tile(2 * m + 1 - NCH)
-
-        @pl.when(m == NCH // 2 + 2)
-        def _():
-            job_out_a.s1()
-            job_self.s5()
-
+            ar_b(2, m)
+
+    loop(NCH // 2, NCH, lambda c: ar_send(2, c))
     loop(0, NCH, seventh_chunk)
-    job_in_a.start()
-    late_sends(NCH // 2, NCH)
-
-    for hd in range(HL):
-        waits = [] if hd else [functools.partial(wait_d_o, 1)] + [cp.wait for cp in back_cross]
-        attend_back(
-            hd, r.do.at[1], r.do_o.at[1], r.q, r.qr_c, r.kv, r.p_c, r.pr_c, r.o_c, r.or_c, I, 0, r.dq, 0, r.dkv, 0,
-            (lambda: None) if hd else job_in_a.s1, waits,
-        )
-        if hd == 0:
-            ar_b(2, NCH // 2)
-            ar_b(2, NCH // 2 + 1)
-            job_out_a.s2()
+
+    back_of_cross.other(NCH - 2)
+    back_of_cross.other(NCH - 1)
+    back_of_cross.keys(0)
+    on("cross_keys_0")
+    back_of_cross.keys(1)
+    on("cross_keys_1")
+    loop(NCH // 2, NCH // 2 + 2, late_out)
 
     late_cps[0].wait()
-    loop(0, ICH, lambda k: ar_put(2, k, dot_nt(r.dkv[rows(k)], r.wkvc[...])))
-    loop(0, NCH, lambda k: ar_put(0, k, dot_nt(r.dq[rows(k)], r.wqc[...])))
-    job_self.s6()
-    loop(0, D // LANES, job_cross.tile)
-    job_cross.start()
-    loop(NCH // 2 + 2, NCH, lambda c: ar_b(2, c))
+
+    def put_last(p, k, value, low_ref, gain_row):
+        ar_put(p, k, value)
+        xhat = low_ref[rows(k)].astype(f32) * (1.0 / gains[gain_row : gain_row + 1, :])
+        r.gz[gain_row : gain_row + 1, :] += jnp.sum(value * xhat, axis=0, keepdims=True)
+
+    loop(0, ICH, lambda k: put_last(2, k, dot_nt(r.dkv[rows(k)], r.wkvc[...]), r.bn, 1))
+    loop(0, NCH, lambda k: put_last(0, k, dot_nt(r.dq[rows(k)], r.wqc[...]), r.an, 0))
+
+    def gz_cp(k, where):
+        return remote(r.gz, r.gzr.at[k], r.gz_snd.at[k], r.gz_rcv.at[k], where)
+
+    @pl.when(is_end)
+    def _():
+        gz_cp(0, at_pair).start()
+
+    def gz_one():
+        @pl.when(is_mid)
+        def _():
+            gz_cp(0, at_pair).wait_recv()
+            r.gz[...] += r.gzr[0]
+            gz_cp(1, at_mid).start()
+
+    def gz_two():
+        @pl.when(is_mid)
+        def _():
+            gz_cp(1, at_mid).wait()
+            r.gz[...] += r.gzr[1]
+            gz_cp(2, at_pair).start()
+
+    def gz_three():
+        @pl.when(is_end)
+        def _():
+            gz_cp(0, at_pair).wait_send()
+            gz_cp(2, at_pair).wait_recv()
+            r.dg[0:2, :] = r.gzr[2, 0:2, :]
+
+        @pl.when(is_mid)
+        def _():
+            gz_cp(2, at_pair).wait_send()
+            r.dg[0:2, :] = r.gz[0:2, :]
+
+    def dg_cp(k):
+        return remote(r.dg, r.dgr.at[k], r.dg_snd.at[k], r.dg_rcv.at[k], (at_core, at_x, at_y)[k])
+
+    def dg_next(k):
+        def step():
+            dg_cp(k).wait()
+            r.dg[...] += r.dgr[k]
+            if k < 2:
+                dg_cp(k + 1).start()
+
+        return step
+
+    dg_zero, dg_one, dg_two = (dg_next(k) for k in range(3))
+
+    loop(NCH // 2 + 2, NCH, late_out)
+    late_cps[1].start()
+    on("last_put")
     loop(0, 2, lambda c: ar_b(2, c))
-    job_in_a.s2()
-    job_out_a.s3()
+
+    extra.update(gz1=gz_one, gz2=gz_two, gz3=gz_three, dg0=dg_cp(0).start, dg1=dg_zero, dg2=dg_one, dg3=dg_two)
 
     def input_chunk(m):
         @pl.when(m < ICH - 2)
@@ -1219,12 +1300,17 @@
 
         ar_c(2, m)
         rw = rows(m)
-        r.gin[rw] = norm_grad(total_of(2, m), r.bn, 1, r.rs1, rw)
+        r.gin[rw] = norm_grad(total_of(2, m), r.bn, None, 1, r.rs1, rw).astype(bf16)
+
+        on("input", m)
 
     loop(0, ICH, input_chunk)
-    job_cross.s1()
-    job_in_a.s3()
-    job_out_a.s4()
+    out_cps = [
+        pltpu.make_async_copy(r.gin, r.input_grad, r.out_sem.at[0]),
+        pltpu.make_async_copy(r.rb.at[pl.ds(0, T // 2)], r.latent_grad.at[pl.ds(0, T // 2)], r.out_sem.at[1]),
+        pltpu.make_async_copy(r.rb.at[pl.ds(T // 2, T // 2)], r.latent_grad.at[pl.ds(T // 2, T // 2)], r.out_sem.at[3]),
+    ]
+    out_cps[0].start()
 
     def last_chunk(m):
         @pl.when(m < NCH - 2)
@@ -1233,54 +1319,23 @@
 
         ar_c(0, m, 1)
         rw = rows(m)
-        r.dxs[rw] += norm_grad(total_of(0, m), r.an, 0, r.rs0, rw)
-
-        @pl.when(m < NCH // 2)
-        def _():
-            late_out(m + NCH // 2)
-
-        @pl.when(m == 2)
-        def _():
-            job_cross.s2()
-            job_in_a.s4()
-
-        @pl.when(m == 3)
-        def _():
-            job_out_a.s5()
-
-        @pl.when(m == 5)
-        def _():
-            job_cross.s3()
-            job_in_a.s5()
+        r.rb[rw] = (r.dxs[rw] + norm_grad(total_of(0, m), r.an, None, 0, r.rs0, rw)).astype(bf16)
+
+        @pl.when(m == 4)
+        def _():
+            out_cps[1].start()
+
+        on("last", m)
 
     loop(0, NCH, last_chunk)
-
-    outs = [
-        pltpu.make_async_copy(r.dxs, r.latent_grad, r.out_sem.at[0]),
-        pltpu.make_async_copy(r.gin, r.input_grad, r.out_sem.at[1]),
-        late_cps[1],
-    ]
-    for cp in outs:
-        cp.start()
-    for k, where in enumerate((at_core, at_x, at_y)):
-        cp = remote(r.dg, r.dgr.at[k], r.dg_snd.at[k], r.dg_rcv.at[k], where)
-        cp.start()
-        cp.wait()
-        r.dg[...] += r.dgr[k]
-        if k == 0:
-            job_cross.s4()
-            job_out_a.s6()
+    out_cps[2].start()
     r.gains_grad[...] = r.dg[...]
-    job_cross.s5()
-    job_in_a.s6()
-    job_cross.s6()
-
-    @pl.when(is_mid)
-    def _():
-        loop(0, NCH, lambda c: cp_tot(2, c).wait_send())
-        loop(0, NCH, lambda c: cp_tot(0, c).wait_send())
-
-    for cp in outs:
+    on("end")
+
+    loop(0, NCH, lambda c: drain(2, c))
+    loop(0, NCH, lambda c: drain(0, c))
+
+    for cp in [*out_cps, late_cps[1]]:
         cp.wait()
 
 
@@ -1299,7 +1354,7 @@
     in_any = dict(latents=latents, inputs=inputs, **weights, out_grad=out_grad)
     S = jax.ShapeDtypeStruct
     out_any = dict(
-        latents_out=S((T, D), bf16), latent_grad=S((T, D), f32), input_grad=S((I, D), f32),
+        latents_out=S((T, D), bf16), latent_grad=S((T, D), bf16), input_grad=S((I, D), bf16),
         g_out_b=S((D, F), bf16), g_in_b=S((D, F), bf16), g_self=S((D, 4 * C), bf16),
         g_out_a=S((D, F), bf16), g_in_a=S((D, F), bf16), g_cross=S((D, 4 * C), bf16),
     )
@@ -1314,26 +1369,26 @@
         codes=V((8, I + 2 * T), f32), codes_o=V((8, I + 2 * T), f32),
         qcol=V((T, LANES), f32), qcol_o=V((T, LANES), f32),
         part=V((3, T, D), bf16), rin=V((3, T, D), bf16), rmid=V((3, T, D), bf16),
-        xs=V((T, D), f32), dxs=V((T, D), f32), gin=V((I, D), f32),
+        xs=V((T, D), f32), dxs=V((T, D), f32), gin=V((I, D), bf16),
         an=V((T, D), bf16), bn=V((I, D), bf16), h1=V((T, D), bf16), cs=V((T, D), bf16), h2=V((T, D), bf16),
         rs0=V((T, LANES), f32), rs1=V((I, LANES), f32), rs2=V((T, LANES), f32), rs3=V((T, LANES), f32),
         rs4=V((T, LANES), f32),
         z1=V((T, F), bf16), s1=V((T, F), bf16), du1=V((T, F), bf16), z2=V((T, F), bf16), du2=V((T, F), bf16),
         ra=V((T, D), bf16), rb=V((T, D), bf16),
-        q=V((T, C), bf16), kv=V((2 * I, 2 * C), bf16), p_c=V((HL, T, 2 * I), bf16), o_c=V((T, C), bf16),
-        q2=V((T, C), bf16), kv2=V((2 * T, 2 * C), bf16), p_s=V((HL, T, 2 * T), bf16), o_s=V((T, C), bf16),
-        pr_c=V((HL, T, I), bf16), qr_c=V((T, C), bf16), or_c=V((T, C), bf16),
-        pr_s=V((HL, T, T), bf16), qr_s=V((T, C), bf16), or_s=V((T, C), bf16),
-        do=V((2, T, C), bf16), do_o=V((2, T, C), bf16), ds=V((2 * T, max(T, I)), bf16),
+        q=V((T, C), bf16), kv=V((2 * I, 2 * C), bf16), p_c=V((HL * T, 2 * I), bf16), o_c=V((T, C), bf16),
+        q2=V((T, C), bf16), kv2=V((2 * T, 2 * C), bf16), p_s=V((HL * T, 2 * T), bf16), o_s=V((T, C), bf16),
+        pr_c=V((HL * T, I), bf16), qr_c=V((T, C), bf16), or_c=V((T, C), bf16),
+        pr_s=V((HL * T, T), bf16), qr_s=V((T, C), bf16), or_s=V((T, C), bf16),
+        do=V((2, T, C), bf16), do_o=V((2, T, C), bf16), ds=V((2 * HL * T, max(T, I)), bf16),
         dqkv=V((T, 3 * C), bf16), dq=V((T, C), bf16), dkv=V((I, 2 * C), bf16),
         rc=V((3, half, F), bf16), r1p=V((3, eighth, F), bf16), r1q=V((3, eighth, F), bf16),
         r2p=V((3, piece, F), bf16), r2q=V((3, piece, F), bf16),
-        dg=V((8, D), f32), dgr=V((3, 8, D), f32),
-        load_sem=DMA((16,)), out_sem=DMA((4,)),
+        dg=V((8, D), f32), dgr=V((3, 8, D), f32), gz=V((8, D), f32), gzr=V((3, 8, D), f32),
+        load_sem=DMA((16,)), out_sem=DMA((5,)),
         y_snd=DMA((8,)), y_rcv=DMA((8,)),
-        kv_snd=DMA((NCH,)), kv_rcv=DMA((NCH,)), do_snd=DMA((2, NCH)), do_rcv=DMA((2, NCH)),
-        ar_snd=DMA((3, NCH)), ar_tot=DMA((3, NCH)), ar_in=DMA((3, NCH)), ar_mid=DMA((3, NCH)),
-        j_snd=DMA((6, 10)), j_rcv=DMA((6, 10)), j_own=DMA((6, 2)), dg_snd=DMA((3,)), dg_rcv=DMA((3,)),
+        p_snd=DMA((HL * NCH,)), p_rcv=DMA((HL * NCH,)), kv_snd=DMA((NCH,)), kv_rcv=DMA((NCH,)), do_snd=DMA((2, NCH)), do_rcv=DMA((2, NCH)),
+        ar_snd=DMA((3, 2 * NCH)), ar_tot=DMA((3, 2 * NCH)), ar_in=DMA((3, 2 * NCH)), ar_mid=DMA((3, 2 * NCH)),
+        j_snd=DMA((6, 10)), j_rcv=DMA((6, 10)), j_own=DMA((6, 2)), dg_snd=DMA((3,)), dg_rcv=DMA((3,)), gz_snd=DMA((3,)), gz_rcv=DMA((3,)),
     )
     names = [*in_vmem, *in_any, *out_any, *out_vmem, *scratch]
     outs = pl.pallas_call(
@@ -1354,6 +1409,66 @@
     return dict(zip([*out_any, *out_vmem], outs, strict=True))
 
 
+def widen_kernel(C, n_gains, lat_in, lgrad_in, igrad_in, gains_in, cross, own, in_a, out_a, in_b, out_b,
+                 lat, lgrad, igrad, gains, q, kv, o_c, w_in_a, w_out_a, qkv, o_s, w_in_b, w_out_b):
+    lat[0] = lat_in[...]
+    lgrad[0] = lgrad_in[...].astype(f32)
+    igrad[0] = igrad_in[...].astype(f32)
+    gains[...] = gains_in[0:n_gains, :]
+    for j in range(2):
+        kv[:, j, :] = cross[:, j * C : (j + 1) * C].astype(f32)
+    q[...] = cross[:, 2 * C : 3 * C].astype(f32)
+    o_c[...] = cross[:, 3 * C :].astype(f32)
+    for j in range(3):
+        qkv[j] = own[:, j * C : (j + 1) * C].astype(f32)
+    o_s[...] = own[:, 3 * C :].astype(f32)
+    w_in_a[...] = in_a[...].astype(f32)
+    w_out_a[...] = out_a[...].astype(f32)
+    w_in_b[...] = in_b[...].astype(f32)
+    w_out_b[...] = out_b[...].astype(f32)
+
+
+def widen_call(o, C, n_gains):
+    T, D = o["latents_out"].shape
+    I = o["input_grad"].shape[0]
+    F = o["g_in_a"].shape[1]
+    steps = 8
+    S = jax.ShapeDtypeStruct
+
+    def flat(n, width):
+        return pl.BlockSpec((n // steps, width), lambda i: (i, 0))
+
+    def whole(n, width):
+        return pl.BlockSpec((n, width), lambda i: (0, 0))
+
+    def lead(n, width):
+        return pl.BlockSpec((1, n // steps, width), lambda i: (0, i, 0))
+
+    ins = ["latents_out", "latent_grad", "input_grad", "gains_grad", "g_cross", "g_self", "g_in_a", "g_out_a", "g_in_b", "g_out_b"]
+    big = flat(D, F)
+    col = flat(D, C)
+    outs = pl.pallas_call(
+        functools.partial(widen_kernel, C, n_gains),
+        grid=(steps,),
+        in_specs=[flat(T, D), flat(T, D), flat(I, D), whole(8, D), big, big, big, big, big, big],
+        out_specs=(
+            lead(T, D), lead(T, D), lead(I, D), whole(n_gains, D), col,
+            pl.BlockSpec((D // steps, 2, C), lambda i: (i, 0, 0)), col, big, big,
+            pl.BlockSpec((3, D // steps, C), lambda i: (0, i, 0)), col, big, big,
+        ),
+        out_shape=(
+            S((1, T, D), bf16), S((1, T, D), f32), S((1, I, D), f32), S((n_gains, D), f32), S((D, C), f32),
+            S((D, 2, C), f32), S((D, C), f32), S((D, F), f32), S((D, F), f32),
+            S((3, D, C), f32), S((D, C), f32), S((D, F), f32), S((D, F), f32),
+        ),
+        compiler_params=pltpu.CompilerParams(vmem_limit_bytes=62 * 2**20),
+        name="widen_kernel",
+    )(*[o[n] for n in ins])
+    outs = list(outs)
+    outs[9] = jnp.moveaxis(outs[9], 0, 1)
+    return tuple(outs)
+
+
 def per_device_fast(
     latents, inputs, latent_group, latent_valid, input_group, input_valid, gains,
     w_q_cross, w_kv_cross, w_o_cross, w_in_a, w_out_a, w_qkv_self, w_o_self, w_in_b, w_out_b, out_grad,
@@ -1362,27 +1477,12 @@
     C = w_q_cross.shape[1]
     weights = dict(
         w_q_c=w_q_cross, w_kv_c=w_kv_cross.reshape(D, 2 * C), w_o_c=w_o_cross, w_in_a=w_in_a,
-        w_out_a=w_out_a, w_qkv_s=w_qkv_self.reshape(D, 3 * C), w_o_s=w_o_self, w_in_b=w_in_b, w_out_b=w_out_b,
+        w_out_a=w_out_a, w_qkv_s=jnp.moveaxis(w_qkv_self, 1, 0), w_o_s=w_o_self, w_in_b=w_in_b, w_out_b=w_out_b,
     )
     o = block_call(
         latents[0], inputs[0], latent_group, latent_valid, input_group, input_valid, gains, weights, out_grad[0]
     )
-    g_cross, g_self = o["g_cross"], o["g_self"]
-    return (
-        o["latents_out"][None],
-        o["latent_grad"][None],
-        o["input_grad"][None],
-        o["gains_grad"][: gains.shape[0]],
-        g_cross[:, 2 * C : 3 * C].astype(f32),
-        g_cross[:, : 2 * C].astype(f32).reshape(D, 2, C),
-        g_cross[:, 3 * C :].astype(f32),
-        o["g_in_a"].astype(f32),
-        o["g_out_a"].astype(f32),
-        g_self[:, : 3 * C].astype(f32).reshape(D, 3, C),
-        g_self[:, 3 * C :].astype(f32),
-        o["g_in_b"].astype(f32),
-        o["g_out_b"].astype(f32),
-    )
+    return widen_call(o, C, gains.shape[0])
 
 
 def solution(mesh):

time: 344 us -> 308 us (0.90)
  local copies, waits for them, and re-layouts: 18.9 us -> 2.42 us
  other arithmetic: 14.9 us -> 0 us
  Pallas kernels: 309 us -> 304 us
    pallas_call x1, Pallas kernels: 309 us -> 288 us  [block_call(): pl.pallas_call(functools.partial(block_kernel, names, T, I, D, C, F, CH),...]
    pallas_call x0 -> x1, Pallas kernels: none -> 16.2 us  [widen_call(): pl.pallas_call(functools.partial(widen_kernel, C, n_gains), grid=(steps,)...]
    convert_element_type x5 -> x0, other arithmetic: 13.2 us -> none  [the longest x1 3.26 us: per_device_fast(): g_cross[:, 3 * C:].astype(f32)]
    unnamed x27 -> x1, local copies, waits for them, and re-layouts: 12.6 us -> 2.42 us
    reshape x3 -> x0, local copies, waits for them, and re-layouts: 6.28 us -> none  [the longest x1 2.36 us: per_device_fast(): g_self[:, :3 * C].astype(f32).reshape(D, 3, C)]
where the time goes in v2:
time: 308 us; the launch traced here: 307 us
  Pallas kernels  304 us (99%)
    pallas_call x1, Pallas kernels, block_call(): pl.pallas_call(functools.partial(block_kernel, names, T, I, D, C, F, CH),...  288 us
    pallas_call x1, Pallas kernels, widen_call(): pl.pallas_call(functools.partial(widen_kernel, C, n_gains), grid=(steps,)...  16.2 us

profile of v2, /device:TPU:0, one launch (start us, length us, event | category | flops | bytes accessed | tf_op | source)
XLA Modules:
  0.0 307.1 jit_solution(14414697854797346377)
XLA Ops:
  0.6 2.4 copy.30
  3.1 287.8 %block_kernel.1 = (bf16[512,1024]{1,0:T(8,128)(2,1)}, bf16[512,1024]{1,0:T(8,128)(2,1)}, bf16[256,1024]{1,0:T(8,128)(2,1)}, bf16[1024,1024]{1,0:T(8,128)(2,1)}, ...) custom-call(s32[1,512]{1,0:T(1,128)} %refs_0_.1, ...), custom_call_target="tpu_custom_call" | custom-call | tf_op jit(solution)/shard_map/block_kernel/pallas_call | solution.py:1394
  290.8 16.2 %widen_kernel.1 = (bf16[1,512,1024]{2,1,0:T(8,128)(2,1)}, f32[1,512,1024]{2,1,0:T(8,128)}, f32[1,256,1024]{2,1,0:T(8,128)}, f32[5,1024]{1,0:T(8,128)}, f32[1024,...) custom-call(bf16[512,1024]{1,0:T(8,128)(2,1)} %get-tuple-element.36., ...), custom_call_target="tpu_custom_call" | custom-call | tf_op jit(solution)/shard_map/widen_kernel/pallas_call | solution.py:1450

commit v3 on v2

--- a/solution.py
+++ b/solution.py
@@ -551,18 +551,16 @@
 
 
 SCHEDULE = dict(
-    fifth=["At", "Bt", "A1", "", "B1", "", "", ""],
-    self_keys_0=[""],
-    self_keys_1=["A2"],
-    sixth_put=["B2 St"],
-    sixth=["A3", "B3 S1", "A4", "B4", "S2", "A5", "S3", "B5"],
-    seventh=["Ct S4", "Dt", "C1 A6", "", "D1", "B6", "", ""],
-    cross_keys_0=["C2"],
-    cross_keys_1=["D2 S5"],
-    last_put=["Xt C3 D3"],
-    input=["X1 C4", "gz1 D4", "S6 C5", "gz2 X2"],
-    last=["D5", "X3 gz3 dg0", "C6", "X4 dg1", "D6", "dg2", "X5", "dg3"],
-    end=["X6"],
+    fifth=["At", "Bt", "", "A1", "B1", "", "", ""],
+    sixth_put=["A2 St B2"],
+    sixth=["A3", "S1", "B3", "", "S2 A4", "", "S3 B4", ""],
+    seventh_pre=["Ct Dt"],
+    seventh=["A5", "S4", "B5", "", "C1", "A6 B6", "S5", "D1"],
+    last_put=["C2 Xt"],
+    late_end=["C3 D2 S6"],
+    input=["X1", "C4", "D3", "X2 gz1"],
+    last=["", "gz2 D4", "C5", "X3 gz3 dg0", "dg1", "X4 D5", "dg2", "dg3"],
+    end=["X5 C6 X6 D6"],
 )
 
 
@@ -682,6 +680,11 @@
         r.part[p, rows(c)] = value.astype(bf16)
         ar_send(p, c)
 
+    def ar_put_wide(p, c, value):
+        r.part[p, rows(c, 2 * CH)] = value.astype(bf16)
+        ar_send(p, 2 * c)
+        ar_send(p, 2 * c + 1)
+
     def ar_b(p, c):
         @pl.when(is_mid)
         def _():
@@ -692,6 +695,10 @@
                 cp_mid(p, k).start()
 
     def ar_c(p, c, prev=None):
+        ar_c_mid(p, c, prev)
+        ar_c_end(p, c)
+
+    def ar_c_mid(p, c, prev=None):
         @pl.when(is_mid)
         def _():
             for k in subs(c):
@@ -703,6 +710,7 @@
                     cp_tot(prev, k).wait_send()
                 cp_tot(p, k).start()
 
+    def ar_c_end(p, c):
         @pl.when(is_end)
         def _():
             for k in subs(c):
@@ -842,11 +850,11 @@
         def s6(self):
             self.cp_all().wait()
 
-    job_out_b = Job(0, r.woutb, r.rc.at[0], r.g_out_b, [(r.r4, r.z2)])
+    job_out_b = Job(0, r.wj, r.rc.at[0], r.g_out_b, [(r.r4, r.z2)])
     job_in_b = Job(1, r.winb, r.rc.at[1], r.g_in_b, [(r.h2, r.du2)])
-    job_self = Job(2, r.wj, r.rc.at[2], r.g_self, [(r.cs, r.dqkv), (r.ra, r.o_s)])
-    job_out_a = Job(3, r.p_s, r.z2, r.g_out_a, [(r.rb, r.z1)])
-    job_in_a = Job(4, r.woutb, r.du2, r.g_in_a, [(r.h1, r.du1)])
+    job_self = Job(2, r.woutb, r.rc.at[2], r.g_self, [(r.cs, r.dqkv), (r.ra, r.o_s)])
+    job_out_a = Job(3, r.p_s, r.z2, r.g_out_a, [(r.lat, r.z1)])
+    job_in_a = Job(4, r.wj, r.du2, r.g_in_a, [(r.h1, r.du1)])
     job_cross = Job(5, r.winb, r.h2, r.g_cross, [(r.bn, r.dkv), (r.an, r.dq), (r.ra, r.o_c)])
 
     def norm_out(x, gain_row, out, rstd_out, rw):
@@ -1008,7 +1016,6 @@
         du = (dot_nn(r.r4[rw], r.woutb[...]) * slope).astype(bf16)
         r.du2[rw] = du
         ar_put(1, m, dot_nt(du, r.winb[...]))
-        r.part[2, rw] = dot_nt(z, r.woutb[...]).astype(bf16)
 
         @pl.when(m >= NCH - 2)
         def _():
@@ -1077,19 +1084,27 @@
             def _():
                 self.other(NCH - 3)
 
-        def keys(self, hd):
-            if hd >= HL:
-                return
+        def keys_own(self):
             n = self.n
-            cols = slice(hd * HEAD_DIM, (hd + 1) * HEAD_DIM)
-            at = 2 * hd * T
-            dk = dot_tn(r.ds[at : at + T, 0:n], self.q[:, cols]) + dot_tn(r.ds[at + T : at + 2 * T, 0:n], self.qr[:, cols])
-            col = self.dkv_col + hd * HEAD_DIM
-            self.dkv[:, col : col + HEAD_DIM] = (dk * SCALE).astype(bf16)
-            at = hd * T
-            dv = dot_tn(self.p[at : at + T, 0:n], self.do[:, cols]) + dot_tn(self.pr[at : at + T, :], self.do_o[:, cols])
-            col += C
-            self.dkv[:, col : col + HEAD_DIM] = dv.astype(bf16)
+            out = []
+            for hd in range(HL):
+                cols = slice(hd * HEAD_DIM, (hd + 1) * HEAD_DIM)
+                at = 2 * hd * T
+                dk = dot_tn(r.ds[at : at + T, 0:n], self.q[:, cols])
+                dv = dot_tn(self.p[hd * T : (hd + 1) * T, 0:n], self.do[:, cols])
+                out.append((dk, dv))
+            return out
+
+        def keys(self, own):
+            n = self.n
+            for hd, (dk, dv) in enumerate(own):
+                cols = slice(hd * HEAD_DIM, (hd + 1) * HEAD_DIM)
+                at = (2 * hd + 1) * T
+                dk = dk + dot_tn(r.ds[at : at + T, 0:n], self.qr[:, cols])
+                dv = dv + dot_tn(self.pr[hd * T : (hd + 1) * T, :], self.do_o[:, cols])
+                col = self.dkv_col + hd * HEAD_DIM
+                self.dkv[:, col : col + HEAD_DIM] = (dk * SCALE).astype(bf16)
+                self.dkv[:, col + C : col + C + HEAD_DIM] = dv.astype(bf16)
 
     back_of_self = Back(0, r.q2, r.qr_s, r.kv2, r.p_s, r.pr_s, r.o_s, r.or_s, T, I, r.dqkv, r.dqkv, C)
     back_of_cross = Back(1, r.q, r.qr_c, r.kv, r.p_c, r.pr_c, r.o_c, r.or_c, I, 0, r.dq, r.dkv, 0)
@@ -1128,6 +1143,17 @@
         r.ra[rw] = low
         r.do[0, rw] = dot_nn(low, r.wos[...]).astype(bf16)
         d_o_cp(0, m).start()
+
+        @pl.when(m < NCH // 2)
+        def _():
+            wide = rows(m, 2 * CH)
+            r.part[2, wide] = dot_nt(r.z2[wide], r.woutb[...]).astype(bf16)
+
+        @pl.when(m < NCH // 4)
+        def _():
+            ar_send(2, 2 * m)
+            ar_send(2, 2 * m + 1)
+
         back_of_self.own(m)
         back_of_self.some_other(m, [q_back.wait, o_back.wait, lambda: loop(0, HL * NCH, lambda c: p_cp(c).wait())])
 
@@ -1137,57 +1163,56 @@
         def _():
             ar_b(2, m - NCH // 2)
 
-    loop(0, NCH // 2, lambda c: ar_send(2, c))
     loop(0, NCH, fifth_chunk)
 
     def late_out(c):
-        ar_c(2, c)
+        ar_c_end(2, c)
         rw = rows(c)
         r.part[2, rw] = (r.xs[rw] + total_of(2, c)).astype(bf16)
 
+    self_keys = back_of_self.keys_own()
     back_of_self.other(NCH - 2)
     back_of_self.other(NCH - 1)
-    back_of_self.keys(0)
-    on("self_keys_0")
-    loop(0, 2, late_out)
-    back_of_self.keys(1)
-    on("self_keys_1")
-    loop(2, NCH // 2, late_out)
+    back_of_self.keys(self_keys)
+    def sixth_put(k):
+        ar_put_wide(0, k, dot_nt(r.dqkv[rows(k, 2 * CH)], r.wqkvs[...]))
+
+    loop(0, NCH // 2, sixth_put)
+    loop(0, NCH // 2, lambda c: ar_c_mid(2, c))
+    on("sixth_put")
+    loop(0, 2, lambda c: ar_b(0, c))
+
+    def sixth_chunk(m):
+        @pl.when(m < NCH - 2)
+        def _():
+            ar_b(0, m + 2)
+
+        ar_c(0, m, 1)
+        rw = rows(m)
+        dx = r.dxs[rw] + norm_grad(total_of(0, m), r.cs, 3, 3, r.rs3, rw)
+        r.dxs[rw] = dx
+        low = dx.astype(bf16)
+        r.lat[rw] = low
+        du = (dot_nn(low, r.wouta[...]) * r.s1[rw].astype(f32)).astype(bf16)
+        r.du1[rw] = du
+        ar_put(1, m, dot_nt(du, r.wina[...]))
+
+        @pl.when(m >= NCH - 2)
+        def _():
+            ar_b(1, m + 2 - NCH)
+
+        @pl.when(m < NCH // 2)
+        def _():
+            late_out(m)
+
+        on("sixth", m)
+
+    loop(0, NCH, sixth_chunk)
     late_cps = [
         pltpu.make_async_copy(r.part.at[2, rw], r.latents_out.at[rw], r.out_sem.at[2 + 2 * k])
         for k, rw in enumerate([pl.ds(0, T // 2), pl.ds(T // 2, T // 2)])
     ]
     late_cps[0].start()
-
-    def sixth_put(k):
-        ar_put(0, k, dot_nt(r.dqkv[rows(k)], r.wqkvs[...]))
-
-    loop(0, NCH, sixth_put)
-    on("sixth_put")
-    loop(0, 2, lambda c: ar_b(0, c))
-
-    def sixth_chunk(m):
-        @pl.when(m < NCH - 2)
-        def _():
-            ar_b(0, m + 2)
-
-        ar_c(0, m, 1)
-        rw = rows(m)
-        dx = r.dxs[rw] + norm_grad(total_of(0, m), r.cs, 3, 3, r.rs3, rw)
-        r.dxs[rw] = dx
-        low = dx.astype(bf16)
-        r.rb[rw] = low
-        du = (dot_nn(low, r.wouta[...]) * r.s1[rw].astype(f32)).astype(bf16)
-        r.du1[rw] = du
-        ar_put(1, m, dot_nt(du, r.wina[...]))
-
-        @pl.when(m >= NCH - 2)
-        def _():
-            ar_b(1, m + 2 - NCH)
-
-        on("sixth", m)
-
-    loop(0, NCH, sixth_chunk)
     def seventh_chunk(m):
         @pl.when(m < NCH - 2)
         def _():
@@ -1214,26 +1239,24 @@
         def _():
             ar_b(2, m)
 
+    on("seventh_pre")
     loop(NCH // 2, NCH, lambda c: ar_send(2, c))
     loop(0, NCH, seventh_chunk)
 
+    cross_keys = back_of_cross.keys_own()
     back_of_cross.other(NCH - 2)
     back_of_cross.other(NCH - 1)
-    back_of_cross.keys(0)
-    on("cross_keys_0")
-    back_of_cross.keys(1)
-    on("cross_keys_1")
-    loop(NCH // 2, NCH // 2 + 2, late_out)
+    back_of_cross.keys(cross_keys)
 
     late_cps[0].wait()
 
     def put_last(p, k, value, low_ref, gain_row):
-        ar_put(p, k, value)
-        xhat = low_ref[rows(k)].astype(f32) * (1.0 / gains[gain_row : gain_row + 1, :])
+        ar_put_wide(p, k, value)
+        xhat = low_ref[rows(k, 2 * CH)].astype(f32) * (1.0 / gains[gain_row : gain_row + 1, :])
         r.gz[gain_row : gain_row + 1, :] += jnp.sum(value * xhat, axis=0, keepdims=True)
 
-    loop(0, ICH, lambda k: put_last(2, k, dot_nt(r.dkv[rows(k)], r.wkvc[...]), r.bn, 1))
-    loop(0, NCH, lambda k: put_last(0, k, dot_nt(r.dq[rows(k)], r.wqc[...]), r.an, 0))
+    loop(0, ICH // 2, lambda k: put_last(2, k, dot_nt(r.dkv[rows(k, 2 * CH)], r.wkvc[...]), r.bn, 1))
+    loop(0, NCH // 2, lambda k: put_last(0, k, dot_nt(r.dq[rows(k, 2 * CH)], r.wqc[...]), r.an, 0))
 
     def gz_cp(k, where):
         return remote(r.gz, r.gzr.at[k], r.gz_snd.at[k], r.gz_rcv.at[k], where)
@@ -1282,9 +1305,9 @@
 
     dg_zero, dg_one, dg_two = (dg_next(k) for k in range(3))
 
-    loop(NCH // 2 + 2, NCH, late_out)
-    late_cps[1].start()
     on("last_put")
+    loop(NCH // 2, NCH, lambda c: ar_c_mid(2, c))
+    on("late_end")
     loop(0, 2, lambda c: ar_b(2, c))
 
     extra.update(gz1=gz_one, gz2=gz_two, gz3=gz_three, dg0=dg_cp(0).start, dg1=dg_zero, dg2=dg_one, dg3=dg_two)
@@ -1300,17 +1323,19 @@
 
         ar_c(2, m)
         rw = rows(m)
-        r.gin[rw] = norm_grad(total_of(2, m), r.bn, None, 1, r.rs1, rw).astype(bf16)
-
+        r.inp[rw] = norm_grad(total_of(2, m), r.bn, None, 1, r.rs1, rw).astype(bf16)
+
+        late_out(m + NCH // 2)
         on("input", m)
 
     loop(0, ICH, input_chunk)
     out_cps = [
-        pltpu.make_async_copy(r.gin, r.input_grad, r.out_sem.at[0]),
-        pltpu.make_async_copy(r.rb.at[pl.ds(0, T // 2)], r.latent_grad.at[pl.ds(0, T // 2)], r.out_sem.at[1]),
-        pltpu.make_async_copy(r.rb.at[pl.ds(T // 2, T // 2)], r.latent_grad.at[pl.ds(T // 2, T // 2)], r.out_sem.at[3]),
+        pltpu.make_async_copy(r.inp, r.input_grad, r.out_sem.at[0]),
+        pltpu.make_async_copy(r.lat.at[pl.ds(0, T // 2)], r.latent_grad.at[pl.ds(0, T // 2)], r.out_sem.at[1]),
+        pltpu.make_async_copy(r.lat.at[pl.ds(T // 2, T // 2)], r.latent_grad.at[pl.ds(T // 2, T // 2)], r.out_sem.at[3]),
     ]
     out_cps[0].start()
+    late_cps[1].start()
 
     def last_chunk(m):
         @pl.when(m < NCH - 2)
@@ -1319,7 +1344,7 @@
 
         ar_c(0, m, 1)
         rw = rows(m)
-        r.rb[rw] = (r.dxs[rw] + norm_grad(total_of(0, m), r.an, None, 0, r.rs0, rw)).astype(bf16)
+        r.lat[rw] = (r.dxs[rw] + norm_grad(total_of(0, m), r.an, None, 0, r.rs0, rw)).astype(bf16)
 
         @pl.when(m == 4)
         def _():
@@ -1369,12 +1394,12 @@
         codes=V((8, I + 2 * T), f32), codes_o=V((8, I + 2 * T), f32),
         qcol=V((T, LANES), f32), qcol_o=V((T, LANES), f32),
         part=V((3, T, D), bf16), rin=V((3, T, D), bf16), rmid=V((3, T, D), bf16),
-        xs=V((T, D), f32), dxs=V((T, D), f32), gin=V((I, D), bf16),
+        xs=V((T, D), f32), dxs=V((T, D), f32),
         an=V((T, D), bf16), bn=V((I, D), bf16), h1=V((T, D), bf16), cs=V((T, D), bf16), h2=V((T, D), bf16),
         rs0=V((T, LANES), f32), rs1=V((I, LANES), f32), rs2=V((T, LANES), f32), rs3=V((T, LANES), f32),
         rs4=V((T, LANES), f32),
         z1=V((T, F), bf16), s1=V((T, F), bf16), du1=V((T, F), bf16), z2=V((T, F), bf16), du2=V((T, F), bf16),
-        ra=V((T, D), bf16), rb=V((T, D), bf16),
+        ra=V((T, D), bf16),
         q=V((T, C), bf16), kv=V((2 * I, 2 * C), bf16), p_c=V((HL * T, 2 * I), bf16), o_c=V((T, C), bf16),
         q2=V((T, C), bf16), kv2=V((2 * T, 2 * C), bf16), p_s=V((HL * T, 2 * T), bf16), o_s=V((T, C), bf16),
         pr_c=V((HL * T, I), bf16), qr_c=V((T, C), bf16), or_c=V((T, C), bf16),
@@ -1402,7 +1427,7 @@
         ),
         scratch_shapes=list(scratch.values()),
         compiler_params=pltpu.CompilerParams(
-            collective_id=0, has_side_effects=True, vmem_limit_bytes=63 * 2**20
+            collective_id=0, has_side_effects=True, vmem_limit_bytes=66900000
         ),
         name="block_kernel",
     )(*in_vmem.values(), *in_any.values())
@@ -1432,7 +1457,7 @@
     T, D = o["latents_out"].shape
     I = o["input_grad"].shape[0]
     F = o["g_in_a"].shape[1]
-    steps = 8
+    steps = 4
     S = jax.ShapeDtypeStruct
 
     def flat(n, width):

time: 308 us -> 285 us (0.925)
  Pallas kernels: 304 us -> 281 us
    pallas_call x1, Pallas kernels: 288 us -> 267 us  [block_call(): pl.pallas_call(functools.partial(block_kernel, names, T, I, D, C, F, CH),...]
where the time goes in v3:
time: 285 us
  Pallas kernels  281 us (99%)
    pallas_call x1, Pallas kernels, block_call(): pl.pallas_call(functools.partial(block_kernel, names, T, I, D, C, F, CH),...  267 us
    pallas_call x1, Pallas kernels, widen_call(): pl.pallas_call(functools.partial(widen_kernel, C, n_gains), grid=(steps,)...  14.8 us

profile of v3, /device:TPU:0, one launch (start us, length us, event | category | flops | bytes accessed | tf_op | source)
XLA Modules:
  0.0 284.7 jit_solution(9308741680591750083)
XLA Ops:
  0.6 2.4 copy.30
  3.1 266.6 %block_kernel.1 = (bf16[512,1024]{1,0:T(8,128)(2,1)}, bf16[512,1024]{1,0:T(8,128)(2,1)}, bf16[256,1024]{1,0:T(8,128)(2,1)}, bf16[1024,1024]{1,0:T(8,128)(2,1)}, ...) custom-call(s32[1,512]{1,0:T(1,128)} %refs_0_.1, ...), custom_call_target="tpu_custom_call" | custom-call | tf_op jit(solution)/shard_map/block_kernel/pallas_call | solution.py:1419
  269.7 14.8 %widen_kernel.1 = (bf16[1,512,1024]{2,1,0:T(8,128)(2,1)}, f32[1,512,1024]{2,1,0:T(8,128)}, f32[1,256,1024]{2,1,0:T(8,128)}, f32[5,1024]{1,0:T(8,128)}, f32[1024,...) custom-call(bf16[512,1024]{1,0:T(8,128)(2,1)} %get-tuple-element.36., ...), custom_call_target="tpu_custom_call" | custom-call | tf_op jit(solution)/shard_map/widen_kernel/pallas_call | solution.py:1475

commit v4 on v3

--- a/solution.py
+++ b/solution.py
@@ -552,15 +552,15 @@
 
 SCHEDULE = dict(
     fifth=["At", "Bt", "", "A1", "B1", "", "", ""],
-    sixth_put=["A2 St B2"],
+    sixth_put=["St A2 B2"],
     sixth=["A3", "S1", "B3", "", "S2 A4", "", "S3 B4", ""],
     seventh_pre=["Ct Dt"],
-    seventh=["A5", "S4", "B5", "", "C1", "A6 B6", "S5", "D1"],
-    last_put=["C2 Xt"],
+    seventh=["A5", "S4", "B5", "", "", "C1 A6 B6", "S5", "D1"],
+    last_put=["Xt C2"],
     late_end=["C3 D2 S6"],
     input=["X1", "C4", "D3", "X2 gz1"],
-    last=["", "gz2 D4", "C5", "X3 gz3 dg0", "dg1", "X4 D5", "dg2", "dg3"],
-    end=["X5 C6 X6 D6"],
+    last=["", "gz2", "X3 D4", "C5 gz3 dg0", "X4 dg1", "", "D5 dg2", "X5 dg3"],
+    end=["C6 X6 D6"],
 )
 
 
@@ -652,7 +652,7 @@
     codes_cp = to_y(r.codes, r.codes_o, 0)
     codes_cp.start()
 
-    SUB = 2
+    SUB = 4
     SR = CH // SUB
 
     def cp_in(p, c):
@@ -882,9 +882,11 @@
         low = norm_out(r.inp[rw].astype(f32), 1, r.bn, r.rs1, rw)
         r.kv[rw] = dot_nn(low, r.wkvc[...]).astype(bf16)
 
-    loop(0, I // LANES, kv_chunk)
-    kv_cp = to_y(r.kv.at[pl.ds(0, I)], r.kv.at[pl.ds(I, I)], 1)
-    kv_cp.start()
+    kv_cps = [to_y(r.kv.at[pl.ds(k * I // 2, I // 2)], r.kv.at[pl.ds(I + k * I // 2, I // 2)], (1, 5)[k]) for k in range(2)]
+    for k in range(2):
+        loop(k * (I // LANES // 2), (k + 1) * (I // LANES // 2), kv_chunk)
+        kv_cps[k].start()
+
     loads["lat"].wait()
     loads["wqc"].wait()
 
@@ -896,7 +898,8 @@
     loop(0, T // LANES, q_chunk)
     codes_cp.wait()
     make_columns(r.codes_o[0:1, I + T : I + 2 * T], r.qcol_o)
-    kv_cp.wait()
+    for cp in kv_cps:
+        cp.wait()
     loads["woc"].wait()
 
     def attend_chunk(k, q_ref, kv_ref, p_ref, o_ref, start, n):
@@ -1412,7 +1415,7 @@
         load_sem=DMA((16,)), out_sem=DMA((5,)),
         y_snd=DMA((8,)), y_rcv=DMA((8,)),
         p_snd=DMA((HL * NCH,)), p_rcv=DMA((HL * NCH,)), kv_snd=DMA((NCH,)), kv_rcv=DMA((NCH,)), do_snd=DMA((2, NCH)), do_rcv=DMA((2, NCH)),
-        ar_snd=DMA((3, 2 * NCH)), ar_tot=DMA((3, 2 * NCH)), ar_in=DMA((3, 2 * NCH)), ar_mid=DMA((3, 2 * NCH)),
+        ar_snd=DMA((3, 4 * NCH)), ar_tot=DMA((3, 4 * NCH)), ar_in=DMA((3, 4 * NCH)), ar_mid=DMA((3, 4 * NCH)),
         j_snd=DMA((6, 10)), j_rcv=DMA((6, 10)), j_own=DMA((6, 2)), dg_snd=DMA((3,)), dg_rcv=DMA((3,)), gz_snd=DMA((3,)), gz_rcv=DMA((3,)),
     )
     names = [*in_vmem, *in_any, *out_any, *out_vmem, *scratch]

time: 285 us -> 282 us (0.989)
    pallas_call x1, Pallas kernels: 267 us -> 264 us  [block_call(): pl.pallas_call(functools.partial(block_kernel, names, T, I, D, C, F, CH),...]
where the time goes in v4:
time: 282 us
  Pallas kernels  279 us (99%)
    pallas_call x1, Pallas kernels, block_call(): pl.pallas_call(functools.partial(block_kernel, names, T, I, D, C, F, CH),...  264 us
    pallas_call x1, Pallas kernels, widen_call(): pl.pallas_call(functools.partial(widen_kernel, C, n_gains), grid=(steps,)...  14.8 us

profile of v4, /device:TPU:0, one launch (start us, length us, event | category | flops | bytes accessed | tf_op | source)
XLA Modules:
  0.0 281.7 jit_solution(12673100181470153833)
XLA Ops:
  0.6 2.4 copy.30
  3.1 263.7 %block_kernel.1 = (bf16[512,1024]{1,0:T(8,128)(2,1)}, bf16[512,1024]{1,0:T(8,128)(2,1)}, bf16[256,1024]{1,0:T(8,128)(2,1)}, bf16[1024,1024]{1,0:T(8,128)(2,1)}, ...) custom-call(s32[1,512]{1,0:T(1,128)} %refs_0_.1, ...), custom_call_target="tpu_custom_call" | custom-call | tf_op jit(solution)/shard_map/block_kernel/pallas_call | solution.py:1422
  266.8 14.8 %widen_kernel.1 = (bf16[1,512,1024]{2,1,0:T(8,128)(2,1)}, f32[1,512,1024]{2,1,0:T(8,128)}, f32[1,256,1024]{2,1,0:T(8,128)}, f32[5,1024]{1,0:T(8,128)}, f32[1024,...) custom-call(bf16[512,1024]{1,0:T(8,128)(2,1)} %get-tuple-element.36., ...), custom_call_target="tpu_custom_call" | custom-call | tf_op jit(solution)/shard_map/widen_kernel/pallas_call | solution.py:1478

commit v5 on v4

--- a/solution.py
+++ b/solution.py
@@ -977,6 +977,14 @@
         kv2_cp(m).start()
 
     loop(0, NCH, second_chunk)
+    loads["woutb"].wait()
+    loads["r4"].wait()
+
+    def hidden_grad(k):
+        rw = rows(k, TILE)
+        r.du2[rw] = dot_nn(r.r4[rw], r.woutb[...]).astype(bf16)
+
+    loop(0, T // TILE, hidden_grad)
     loop(0, NCH, lambda c: kv2_cp(c).wait())
 
     def p_cp(c):
@@ -1000,8 +1008,6 @@
     o_back = to_y(r.o_s, r.or_s, 7)
     o_back.start()
     loads["winb"].wait()
-    loads["woutb"].wait()
-    loads["r4"].wait()
 
     def third_chunk(m):
         @pl.when((m >= 2) & (m < NCH - 2))
@@ -1016,9 +1022,14 @@
         z, slope = gelu_both(dot_nn(low, r.winb[...]))
         z = z.astype(bf16)
         r.z2[rw] = z
-        du = (dot_nn(r.r4[rw], r.woutb[...]) * slope).astype(bf16)
+        du = (r.du2[rw].astype(f32) * slope).astype(bf16)
         r.du2[rw] = du
         ar_put(1, m, dot_nt(du, r.winb[...]))
+
+        @pl.when((m == 3) | (m == 5))
+        def _():
+            wide = rows((m - 3) // 2, 2 * CH)
+            r.part[2, wide] = dot_nt(r.z2[wide], r.woutb[...]).astype(bf16)
 
         @pl.when(m >= NCH - 2)
         def _():
@@ -1147,7 +1158,7 @@
         r.do[0, rw] = dot_nn(low, r.wos[...]).astype(bf16)
         d_o_cp(0, m).start()
 
-        @pl.when(m < NCH // 2)
+        @pl.when((m >= NCH // 4) & (m < NCH // 2))
         def _():
             wide = rows(m, 2 * CH)
             r.part[2, wide] = dot_nt(r.z2[wide], r.woutb[...]).astype(bf16)
@@ -1460,7 +1471,7 @@
     T, D = o["latents_out"].shape
     I = o["input_grad"].shape[0]
     F = o["g_in_a"].shape[1]
-    steps = 4
+    steps = 2
     S = jax.ShapeDtypeStruct
 
     def flat(n, width):

time: 282 us -> 281 us (level)
  no operation moved by 1% of the time
where the time goes in v5:
time: 281 us
  Pallas kernels  277 us (99%)
    pallas_call x1, Pallas kernels, block_call(): pl.pallas_call(functools.partial(block_kernel, names, T, I, D, C, F, CH),...  263 us
    pallas_call x1, Pallas kernels, widen_call(): pl.pallas_call(functools.partial(widen_kernel, C, n_gains), grid=(steps,)...  14.5 us

profile of v5, /device:TPU:0, one launch (start us, length us, event | category | flops | bytes accessed | tf_op | source)
XLA Modules:
  0.0 280.6 jit_solution(1308198572267675786)
XLA Ops:
  0.6 2.4 copy.30
  3.1 262.8 %block_kernel.1 = (bf16[512,1024]{1,0:T(8,128)(2,1)}, bf16[512,1024]{1,0:T(8,128)(2,1)}, bf16[256,1024]{1,0:T(8,128)(2,1)}, bf16[1024,1024]{1,0:T(8,128)(2,1)}, ...) custom-call(s32[1,512]{1,0:T(1,128)} %refs_0_.1, ...), custom_call_target="tpu_custom_call" | custom-call | tf_op jit(solution)/shard_map/block_kernel/pallas_call | solution.py:1433
  265.9 14.5 %widen_kernel.1 = (bf16[1,512,1024]{2,1,0:T(8,128)(2,1)}, f32[1,512,1024]{2,1,0:T(8,128)}, f32[1,256,1024]{2,1,0:T(8,128)}, f32[5,1024]{1,0:T(8,128)}, f32[1024,...) custom-call(bf16[512,1024]{1,0:T(8,128)(2,1)} %get-tuple-element.36., ...), custom_call_target="tpu_custom_call" | custom-call | tf_op jit(solution)/shard_map/widen_kernel/pallas_call | solution.py:1489
